TPU v7x, 512 devices: a whole 4x8x8 slice. The times are simulated.
512 devices in a mesh: nodes: 64 (over y_hi, z, core), heads: 8 (over x, y_lo).
Axes of the slice: x: 4, y: 8 (y_hi: 4, y_lo: 2; y = y_hi * 2 + y_lo), z: 8, core: 2. Of those that a mesh axis runs over, the one named last changes fastest.
Arguments:
- inputs: bfloat16 [16384, 1024], P('nodes', 'heads'), may hold values from -6 to 6
- out_grad: bfloat16 [16384, 1024], P('nodes', 'heads'), may hold values from -6 to 6
- w_query: bfloat16 [1024, 1024], P(None, 'heads'), may hold values from -0.1875 to 0.1875
- w_key: bfloat16 [1024, 1024], P(None, 'heads'), may hold values from -0.1875 to 0.1875
- w_value: bfloat16 [1024, 1024], P(None, 'heads'), may hold values from -0.1875 to 0.1875
- w_out: bfloat16 [1024, 1024], P('heads'), may hold values from -0.1875 to 0.1875
- live_rows: int32 [64], P('nodes'), may hold values from 85 to 256, as said below
- window_blocks: int32 [128, 3], P('nodes'), may hold values from 0 to 127, as said below
Outputs:
- input_grad: bfloat16 [16384, 1024], P('nodes', 'heads')
- grad_query: bfloat16 [1024, 1024], P(None, 'heads')
- grad_key: bfloat16 [1024, 1024], P(None, 'heads')
- grad_value: bfloat16 [1024, 1024], P(None, 'heads')
- grad_out: bfloat16 [1024, 1024], P('heads')
Inputs may be any that keep to these rules, and one draw needn't show every extreme that they name: `live_rows`: partition 0 and one other partition are full in every draw. `window_blocks`: entry 0 of block b's window is b itself; the other entries are distinct blocks other than b within 2 blocks of b.
All inputs are finite; a program needn't handle non-finite values.
Results may differ from a plain program's by a relative error of at most 0.012.
Values may be sent and summed in bfloat16 or wider, within the bound.
A program may use at most 64 MiB of HBM per device.

v0:
```python
import jax
import jax.numpy as jnp
from jax import lax
from jax.sharding import PartitionSpec as P

HEAD_DIM = 64
BLOCK = 128
HALO_BLOCKS = 2
WINDOW = 3


def extended(array, sides, width):
    for axis, dim in sides:
        count, length = (lax.axis_size(axis), array.shape[dim])
        up = [(i, (i + 1) % count) for i in range(count - 1)]
        down = [(j, i) for i, j in up]
        last = lax.slice_in_dim(array, length - width, length, axis=dim)
        initial = lax.slice_in_dim(array, 0, width, axis=dim)
        before = lax.ppermute(last, axis, up)
        after = lax.ppermute(initial, axis, down)
        array = jnp.concatenate([before, array, after], axis=dim)
    return array


def shifted(array, axis, by):
    count = lax.axis_size(axis)
    pairs = [(i, i + by) for i in range(count) if 0 <= i + by < count]
    return lax.ppermute(array, axis, pairs)


def body(inputs, out_grad, w_query, w_key, w_value, w_out, live_rows, window_blocks):
    scale = HEAD_DIM ** (-0.5)
    row_count = inputs.shape[0]
    col_count = w_query.shape[1]
    head_count = col_count // HEAD_DIM
    blocks_dev = row_count // BLOCK
    rim_rows = HALO_BLOCKS * BLOCK
    ext_blocks = blocks_dev + 2 * HALO_BLOCKS
    ext_rows = ext_blocks * BLOCK
    my_index = lax.axis_index("nodes")
    kv_weights = jnp.concatenate([w_key, w_value], 1)
    grad_full = lax.all_gather(out_grad, "heads", axis=1, tiled=True)
    sizes_near = extended(live_rows, (("nodes", 0),), 1)
    input_full = lax.all_gather(inputs, "heads", axis=1, tiled=True)
    kv_own = jnp.dot(input_full, kv_weights, preferred_element_type=jnp.float32).astype(
        jnp.bfloat16
    )
    kv_ext = extended(kv_own, (("nodes", 0),), rim_rows)
    queries = jnp.dot(input_full, w_query, preferred_element_type=jnp.float32).astype(jnp.bfloat16)
    back = lax.dot_general(
        grad_full, w_out, (((1,), (1,)), ((), ())), preferred_element_type=jnp.float32
    ).astype(jnp.bfloat16)
    ext_local = jnp.arange(ext_rows, dtype=jnp.int32) - rim_rows
    relative = (ext_local + row_count) // row_count
    owner_size = jnp.sum(
        jnp.where(
            relative[:, None] == jnp.arange(3, dtype=jnp.int32)[None, :], sizes_near[None, :], 0
        ),
        1,
    )
    live_ext = ext_local - (relative - 1) * row_count < owner_size
    local_ids = window_blocks - (my_index * blocks_dev - HALO_BLOCKS)
    kv_sel = kv_ext.reshape(ext_blocks, BLOCK, 2 * col_count)[local_ids].reshape(
        blocks_dev, WINDOW * BLOCK, 2 * col_count
    )
    key_sel = kv_sel[:, :, :col_count].reshape(blocks_dev, WINDOW * BLOCK, head_count, HEAD_DIM)
    val_sel = kv_sel[:, :, col_count:].reshape(blocks_dev, WINDOW * BLOCK, head_count, HEAD_DIM)
    live_sel = live_ext.reshape(ext_blocks, BLOCK)[local_ids].reshape(blocks_dev, WINDOW * BLOCK)
    block_pos = jnp.arange(BLOCK, dtype=jnp.int32)
    key_pos = (local_ids[:, :, None] * BLOCK + block_pos[None, None, :]).reshape(
        blocks_dev, WINDOW * BLOCK
    )
    query_pos = (
        rim_rows + jnp.arange(blocks_dev, dtype=jnp.int32)[:, None] * BLOCK + block_pos[None, :]
    )
    allowed = live_sel[:, None, :] | (key_pos[:, None, :] == query_pos[:, :, None])
    query_blk = queries.reshape(blocks_dev, BLOCK, head_count, HEAD_DIM)
    back_blk = back.reshape(blocks_dev, BLOCK, head_count, HEAD_DIM)
    scores = (
        jnp.einsum("bqhd,bkhd->bhqk", query_blk, key_sel, preferred_element_type=jnp.float32)
        * scale
    )
    expo = jnp.where(allowed[:, None], jnp.exp(scores), 0.0)
    probs = expo / jnp.sum(expo, -1, keepdims=True)
    probs_low = probs.astype(jnp.bfloat16)
    attended = jnp.einsum("bhqk,bkhd->bqhd", probs_low, val_sel, preferred_element_type=jnp.float32)
    attn_low = attended.reshape(row_count, col_count).astype(jnp.bfloat16)
    out_term = lax.dot_general(
        attn_low, grad_full, (((0,), (0,)), ((), ())), preferred_element_type=jnp.float32
    )
    dprob = jnp.einsum("bqhd,bkhd->bhqk", back_blk, val_sel, preferred_element_type=jnp.float32)
    delta = jnp.sum(probs * dprob, -1, keepdims=True)
    dscore = (scale * probs * (dprob - delta)).astype(jnp.bfloat16)
    dquery = jnp.einsum("bhqk,bkhd->bqhd", dscore, key_sel, preferred_element_type=jnp.float32)
    dkey = jnp.einsum("bhqk,bqhd->bkhd", dscore, query_blk, preferred_element_type=jnp.float32)
    dval = jnp.einsum("bhqk,bqhd->bkhd", probs_low, back_blk, preferred_element_type=jnp.float32)
    dkv_sel = jnp.concatenate(
        [
            dkey.reshape(blocks_dev, WINDOW, BLOCK, col_count),
            dval.reshape(blocks_dev, WINDOW, BLOCK, col_count),
        ],
        -1,
    )
    dkv_sel = dkv_sel.reshape(blocks_dev * WINDOW, BLOCK * 2 * col_count)
    one_hot = (
        local_ids.reshape(-1)[:, None] == jnp.arange(ext_blocks, dtype=jnp.int32)[None, :]
    ).astype(jnp.float32)
    dkv_ext = lax.dot_general(
        one_hot,
        dkv_sel,
        (((0,), (0,)), ((), ())),
        precision=lax.Precision.HIGHEST,
        preferred_element_type=jnp.float32,
    ).reshape(ext_rows, 2 * col_count)
    from_high = shifted(dkv_ext[:rim_rows], "nodes", -1)
    from_low = shifted(dkv_ext[ext_rows - rim_rows :], "nodes", 1)
    dkv_own = dkv_ext[rim_rows : rim_rows + row_count]
    dkv_own = dkv_own.at[:rim_rows].add(from_low)
    dkv_own = dkv_own.at[row_count - rim_rows :].add(from_high)
    dq_low = dquery.reshape(row_count, col_count).astype(jnp.bfloat16)
    dkv_low = dkv_own.astype(jnp.bfloat16)
    grads_all = jnp.concatenate([dq_low, dkv_low], 1)
    weights_all = jnp.concatenate([w_query, kv_weights], 1)
    proj_term = lax.dot_general(
        input_full, grads_all, (((0,), (0,)), ((), ())), preferred_element_type=jnp.float32
    )
    input_term = lax.dot_general(
        grads_all, weights_all, (((1,), (1,)), ((), ())), preferred_element_type=jnp.float32
    )
    input_grad = lax.psum_scatter(input_term, "heads", scatter_dimension=1, tiled=True).astype(
        jnp.bfloat16
    )
    proj_total, out_total = lax.psum((proj_term, out_term), "nodes")
    grad_query = proj_total[:, :col_count].astype(jnp.bfloat16)
    grad_key = proj_total[:, col_count : 2 * col_count].astype(jnp.bfloat16)
    grad_value = proj_total[:, 2 * col_count :].astype(jnp.bfloat16)
    grad_out = out_total.astype(jnp.bfloat16)
    return (input_grad, grad_query, grad_key, grad_value, grad_out)


def solution(mesh):
    placed = (
        P("nodes", "heads"),
        P("nodes", "heads"),
        P(None, "heads"),
        P(None, "heads"),
        P(None, "heads"),
        P("heads", None),
        P("nodes"),
        P("nodes", None),
    )
    return jax.shard_map(
        body,
        mesh=mesh,
        in_specs=placed,
        out_specs=(
            P("nodes", "heads"),
            P(None, "heads"),
            P(None, "heads"),
            P(None, "heads"),
            P("heads", None),
        ),
        check_vma=False,
    )
```

profile of v0, /device:TPU:32, one launch (start us, length us, event | category | flops | bytes accessed | tf_op | source)
XLA Modules:
  0.0 429.2 jit_solution(10722700438657104052)
XLA Ops:
  7.2 0.0 copy-start
  7.2 0.0 copy-start.4
  7.2 0.0 reduce-scatter.2.cloned.1.call-start
  7.2 2.1 collective-permute-start.2
  9.3 10.2 %collective-permute-start.3 = (s32[1]{0:T(128)}, s32[1]{0:T(128)}, u32[]{:S(2)}, u32[]{:S(2)}) collective-permute-start(s32[1]{0:T(128)} %param.22), channel_id=1, source_target_pairs={{8,0},{16,8},{24,16},{32,24},{40,32},{48,40},{56,48},{64,56},{72,6... | collective-permute-start | bytes 20 | tf_op jit(solution)/shard_map/ppermute | solution.py:20
  19.5 27.1 %all_gather.6 = bf16[256,1024]{1,0:T(8,128)(2,1)S(1)} all-gather(bf16[256,128]{1,0:T(8,128)(2,1)} %param.16), channel_id=1, replica_groups=mesh['nodes'=64,'heads'=8] {'heads'}, dimensions={1}, use_global_device_ids=true | all-gather | bytes 589824 | tf_op jit(solution)/shard_map/all_gather | solution.py:44
  46.6 1.4 fusion.2
  47.9 1.9 collective-permute-start.1
  49.8 2.4 collective-permute-start
  53.0 0.1 eq.51
  53.0 0.1 iota_add_fusion
  53.1 0.1 reshape.178
  53.2 0.1 broadcast_bitcast_fusion
  53.3 0.3 convolution_convert_fusion.4
  53.6 0.1 reshape.199
  53.7 0.1 copy.39
  53.8 26.7 %all_gather.7 = bf16[256,1024]{1,0:T(8,128)(2,1)S(1)} all-gather(bf16[256,128]{1,0:T(8,128)(2,1)S(1)} %copy-done.6), channel_id=1, replica_groups=mesh['nodes'=64,'heads'=8] {'heads'}, dimensions={1}, use_global_device_ids=true | all-gather | bytes 589824 | tf_op jit(solution)/shard_map/all_gather | solution.py:42
  80.5 0.3 convolution_convert_fusion.3
  80.8 0.1 reshape.200
  80.9 0.1 copy.42
  81.0 1.2 pad_add_fusion
  82.3 0.1 select_reduce_fusion
  82.4 0.6 gather_fusion.1
  83.0 0.1 compare_or_fusion
  83.2 0.6 gather_fusion
  83.7 0.1 fusion.42
  83.8 0.2 copy.59
  84.0 0.2 copy.58
  84.2 0.3 fusion.43
  84.5 0.3 fusion.1
  84.8 1.0 fusion.4
  85.9 1.0 convolution_bitcast_fusion.1
  86.9 0.7 copy.48
  87.6 1.1 reshape.174
  88.8 1.3 multiply_reduce_fusion
  90.1 1.3 multiply_convert_fusion
  91.4 0.2 convolution_bitcast_fusion.2
  91.6 0.9 reshape.173
  92.6 1.3 pad_maximum_fusion
  93.8 0.3 copy.46
  94.1 0.5 copy.61
  94.6 0.8 fusion.30
  95.4 0.3 fusion.40
  95.7 0.9 slice.69
  96.6 0.9 slice.71
  97.6 3.9 collective-permute-start.5
  101.5 1.9 collective-permute-start.4
  103.4 0.2 fusion.18
  103.7 0.3 fusion.3
  104.0 0.1 copy.52
  104.1 0.1 reshape.198
  104.2 0.2 slice.67
  104.5 2.9 collective-permute-done.5
  107.4 7.2 %collective-permute-done.4 = f32[256,256]{1,0:T(8,128)S(1)} collective-permute-done((f32[256,256]{1,0:T(8,128)}, f32[256,256]{1,0:T(8,128)S(1)}, u32[]{:S(2)}, u32[]{:S(2)}) %collective-permute-start.4) | collective-permute-done | bytes 262176 | tf_op jit(solution)/shard_map/ppermute | solution.py:28
  114.6 0.1 add_convert_fusion
  114.6 2.4 fusion.5
  117.0 0.0 reduce-scatter.2.cloned.1.call-update
  117.1 0.4 convolution_bitcast_fusion
  117.4 300.8 %all-reduce.2 = (bf16[1024,384]{0,1:T(8,128)(2,1)S(1)}, bf16[128,1024]{1,0:T(8,128)(2,1)}) all-reduce(f32[1024,384]{0,1:T(8,128)S(1)} %convolution_bitcast_fusion, f32[128,1024]{1,0:T(8,128)S(1)} %fusion.18), channel_id=1, replica_groups=mesh['nodes'=64,'heads'=8] {'nodes'}, use_global_device_ids=true, to_apply=%region_4.5 | all-reduce | flops 524288 | bytes 3145728 | tf_op jit(solution)/shard_map/psum | solution.py:133
  418.2 0.1 fusion.41
  418.3 0.8 copy.51
  419.1 0.8 copy.50
  419.9 0.8 copy.49
  420.8 1.5 convert_element_type.59
  (33 shorter events, 0.2 us)
Async XLA Ops:
  7.2 73.3 %copy-start = (bf16[128,1024]{1,0:T(8,128)(2,1)S(1)}, bf16[128,1024]{1,0:T(8,128)(2,1)}, u32[]{:S(2)}) copy-start(bf16[128,1024]{1,0:T(8,128)(2,1)} %param.21) | copy-start | bytes 786436
  7.2 45.7 %copy-start.8 = (s32[2,3]{1,0:T(2,128)S(1)}, s32[2,3]{1,0:T(2,128)}, u32[]{:S(2)}) copy-start(s32[2,3]{1,0:T(2,128)} %param.23) | copy-start | bytes 76
  7.2 46.1 %copy-start.4 = (bf16[1024,128]{1,0:T(8,128)(2,1)S(1)}, bf16[1024,128]{1,0:T(8,128)(2,1)}, u32[]{:S(2)}) copy-start(bf16[1024,128]{1,0:T(8,128)(2,1)} %param.18) | copy-start | bytes 786436
  7.2 413.6 %reduce-scatter.2.cloned.1.call-start = ((), (), s32[]{:S(2)}) async-start(), calls=%async_computation.1 | async-start | bytes 1179648 | tf_op jit(solution)/shard_map/reduce_scatter | solution.py:130
  7.2 73.7 %collective-permute-start.2 = (s32[1]{0:T(128)}, s32[1]{0:T(128)}, u32[]{:S(2)}, u32[]{:S(2)}) collective-permute-start(s32[1]{0:T(128)} %param.22), channel_id=1, source_target_pairs={{0,8},{8,16},{16,24},{24,32},{32,40},{40,48},{48,56},{56,64},{64,7... | collective-permute-start | bytes 20 | tf_op jit(solution)/shard_map/ppermute | solution.py:19
  9.3 71.7 %collective-permute-start.3 = (s32[1]{0:T(128)}, s32[1]{0:T(128)}, u32[]{:S(2)}, u32[]{:S(2)}) collective-permute-start(s32[1]{0:T(128)} %param.22), channel_id=1, source_target_pairs={{8,0},{16,8},{24,16},{32,24},{40,32},{48,40},{56,48},{64,56},{72,6... | collective-permute-start | bytes 20 | tf_op jit(solution)/shard_map/ppermute | solution.py:20
  46.5 7.2 %copy-start.6 = (bf16[256,128]{1,0:T(8,128)(2,1)S(1)}, bf16[256,128]{1,0:T(8,128)(2,1)}, u32[]{:S(2)}) copy-start(bf16[256,128]{1,0:T(8,128)(2,1)} %param.17) | copy-start | bytes 196612
  47.9 35.2 %collective-permute-start.1 = (bf16[256,256]{1,0:T(8,128)(2,1)S(1)}, bf16[256,256]{1,0:T(8,128)(2,1)S(1)}, u32[]{:S(2)}, u32[]{:S(2)}) collective-permute-start(bf16[256,256]{1,0:T(8,128)(2,1)S(1)} %fusion.2), channel_id=1, source_target_pairs={{8,0},{16,8},{24,16},{32,24},{40,32},{48,40},{56,48},{64,56},{72,6... | collective-permute-start | bytes 393224 | tf_op jit(solution)/shard_map/ppermute | solution.py:20
  49.8 33.3 %collective-permute-start = (bf16[256,256]{1,0:T(8,128)(2,1)S(1)}, bf16[256,256]{1,0:T(8,128)(2,1)S(1)}, u32[]{:S(2)}, u32[]{:S(2)}) collective-permute-start(bf16[256,256]{1,0:T(8,128)(2,1)S(1)} %fusion.2), channel_id=1, source_target_pairs={{0,8},{8,16},{16,24},{24,32},{32,40},{40,48},{48,56},{56,64},{64,7... | collective-permute-start | bytes 393224 | tf_op jit(solution)/shard_map/ppermute | solution.py:19
  84.2 4.6 %copy-start.1 = (bf16[2,384,128]{1,2,0:T(8,128)(2,1)}, bf16[2,384,128]{1,2,0:T(8,128)(2,1)S(1)}, u32[]{:S(2)}) copy-start(bf16[2,384,128]{1,2,0:T(8,128)(2,1)S(1)} %copy.58) | copy-start | bytes 589828
  85.9 1.1 copy-start.7
  95.4 8.0 %copy-start.3 = (bf16[2,128,2,64]{1,0,3,2:T(2,128)(2,1)S(1)}, bf16[2,128,2,64]{1,0,3,2:T(2,128)(2,1)}, u32[]{:S(2)}) copy-start(bf16[2,128,2,64]{1,0,3,2:T(2,128)(2,1)} %copy.48) | copy-start | bytes 196612
  95.4 8.2 %copy-start.2 = (bf16[2,384,128]{1,2,0:T(8,128)(2,1)S(1)}, bf16[2,384,128]{1,2,0:T(8,128)(2,1)}, u32[]{:S(2)}) copy-start(bf16[2,384,128]{1,2,0:T(8,128)(2,1)} %copy-done.1) | copy-start | bytes 589828
  97.6 9.8 %collective-permute-start.5 = (f32[256,256]{1,0:T(8,128)}, f32[256,256]{1,0:T(8,128)S(1)}, u32[]{:S(2)}, u32[]{:S(2)}) collective-permute-start(f32[256,256]{1,0:T(8,128)} %slice.71), channel_id=1, source_target_pairs={{8,0},{16,8},{24,16},{32,24},{40,32},{48,40},{56,48},{64,56},{72,6... | collective-permute-start | bytes 786440 | tf_op jit(solution)/shard_map/ppermute | solution.py:28
  101.5 13.1 %collective-permute-start.4 = (f32[256,256]{1,0:T(8,128)}, f32[256,256]{1,0:T(8,128)S(1)}, u32[]{:S(2)}, u32[]{:S(2)}) collective-permute-start(f32[256,256]{1,0:T(8,128)} %slice.69), channel_id=1, source_target_pairs={{0,8},{8,16},{16,24},{24,32},{32,40},{40,48},{48,56},{56,64},{64,7... | collective-permute-start | bytes 786440 | tf_op jit(solution)/shard_map/ppermute | solution.py:28
  103.7 11.0 %copy-start.5 = (bf16[1024,128]{1,0:T(8,128)(2,1)S(1)}, bf16[1024,128]{1,0:T(8,128)(2,1)}, u32[]{:S(2)}) copy-start(bf16[1024,128]{1,0:T(8,128)(2,1)} %param.18) | copy-start | bytes 786436
  103.7 11.0 %copy-start.9 = (bf16[1024,128]{1,0:T(8,128)(2,1)S(1)}, bf16[1024,128]{1,0:T(8,128)(2,1)}, u32[]{:S(2)}) copy-start(bf16[1024,128]{1,0:T(8,128)(2,1)} %param.20) | copy-start | bytes 786436
Sparse Core Ops, SparseCore 0:
  117.2 41.7 reduce-scatter.1
where the time goes:
time: 430 us; the launch traced here: 429 us
  blocking collectives  354 us (82%)
  starting transfers between devices  22.4 us (5%)
  between operations  15.1 us (4%)
  local copies, waits for them, and re-layouts  11 us (3%)
  matrix products  10.3 us (2%)
  waiting for transfers between devices  10.1 us (2%)
  other arithmetic  5.77 us (1%)
    psum x1, blocking collectives, body(): proj_total, out_total = lax.psum((proj_term, out_term), 'nodes')  301 us
    all_gather x1, blocking collectives, body(): input_full = lax.all_gather(inputs, 'heads', axis=1, tiled=True)  27.1 us
    all_gather x1, blocking collectives, body(): grad_full = lax.all_gather(out_grad, 'heads', axis=1, tiled=True)  26.7 us
    ppermute x2, starting transfers between devices, extended(): after = lax.ppermute(initial, axis, down)  12.1 us
    ppermute x2, waiting for transfers between devices, shifted(): return lax.ppermute(array, axis, pairs)  10.1 us
  transfers between devices with their start and end apart: 7, of which 2 were waited for; matrix products, arithmetic and copies ran while one was open for 2% of the time, Pallas kernels for 0%

commit v1 on v0

v1 whole, which is shorter than its diff:
```python
import functools

import jax
import jax.numpy as jnp
from jax import lax
from jax.experimental import pallas as pl
from jax.experimental.pallas import tpu as pltpu
from jax.sharding import PartitionSpec as P

HEAD_DIM = 64
BLOCK = 128
REACH = 5
ROWS = 256
COLS = 128
SHARDS = 8
NZ = 8
NY = 4
SCALE = HEAD_DIM ** (-0.5)
BF = jnp.bfloat16
F32 = jnp.float32
MESH = pl.DeviceIdType.MESH
NT = (((1,), (1,)), ((), ()))
TN = (((0,), (0,)), ((), ()))


def mm(a, b):
    return jnp.dot(a, b, preferred_element_type=F32)


def mm_nt(a, b):
    return lax.dot_general(a, b, NT, preferred_element_type=F32)


def mm_tn(a, b):
    return lax.dot_general(a, b, TN, preferred_element_type=F32)


class Copies:
    def __init__(self, send, recv):
        self.send, self.recv, self.used, self.started = send, recv, 0, []

    def remote(self, src, dst, device):
        i = self.used
        self.used += 1
        copy = pltpu.make_async_remote_copy(
            src_ref=src,
            dst_ref=dst,
            send_sem=self.send.at[i],
            recv_sem=self.recv.at[i],
            device_id=device,
            device_id_type=MESH,
        )
        copy.start()
        self.started.append(copy)
        return copy


def kernel(
    x_in, g_in, wq_in, wk_in, wv_in, wo_in, live_in, win_in,
    ig_out, f_out,
    xg, gg, wqkv, wo, kv, qm, bm, probs, attn, dq, dkv_ext, dkv_send, dkv_recv, grads,
    terms, core_recv, part, ra1, rb1, sa, sb, ra2, rb2, fin, it_send, it_recv, ig,
    local_sem, send_sem, recv_sem, out_sem,
):
    node = lax.axis_index("nodes")
    head = lax.axis_index("heads")
    core = lax.rem(node, 2)
    z = lax.rem(node // 2, NZ)
    y = node // (2 * NZ)
    nodes = 2 * NZ * NY

    def at_head(d):
        return lax.rem(head + d, SHARDS)

    def at_z(d):
        return lax.rem(z + d, NZ)

    def at_y(d):
        return lax.rem(y + d, NY)

    left = (lax.rem(node + nodes - 1, nodes), head)
    right = (lax.rem(node + 1, nodes), head)
    other = (node + 1 - 2 * core, head)

    def z_dev(d):
        return ((y * NZ + at_z(d)) * 2 + core, head)

    def y_dev(d):
        return ((at_y(d) * NZ + z) * 2 + core, head)

    def head_dev(d):
        return (node, at_head(d))

    partners = [left, right]
    partners += [head_dev(d) for d in range(1, SHARDS)]
    partners += [z_dev(d) for d in range(1, NZ)]
    partners += [y_dev(d) for d in range(1, NY)]
    barrier = pltpu.get_barrier_semaphore()
    for dev in partners:
        pl.semaphore_signal(barrier, inc=1, device_id=dev, device_id_type=MESH)

    loads = [
        pltpu.make_async_copy(x_in, xg.at[head], local_sem.at[0]),
        pltpu.make_async_copy(wq_in, wqkv.at[:, 0:COLS], local_sem.at[1]),
        pltpu.make_async_copy(wk_in, wqkv.at[:, COLS : 2 * COLS], local_sem.at[2]),
        pltpu.make_async_copy(wv_in, wqkv.at[:, 2 * COLS : 3 * COLS], local_sem.at[3]),
        pltpu.make_async_copy(g_in, gg.at[head], local_sem.at[4]),
        pltpu.make_async_copy(wo_in, wo, local_sem.at[5]),
    ]
    for load in loads:
        load.start()

    pl.semaphore_wait(barrier, len(partners))
    copies = Copies(send_sem, recv_sem)
    x_copies = [copies.remote(x_in, xg.at[head], head_dev(d)) for d in range(1, SHARDS)]
    g_copies = [copies.remote(g_in, gg.at[head], head_dev(d)) for d in range(1, SHARDS)]

    live = live_in[0]
    lane_row = lax.broadcasted_iota(jnp.int32, (16, ROWS), 1)
    kv[1, ROWS : ROWS + 16, :] = jnp.where(lane_row < live, 1.0, 0.0).astype(BF)

    for load in loads:
        load.wait()
    for copy in x_copies:
        copy.wait_recv()

    x_full = jnp.concatenate([xg[s] for s in range(SHARDS)], axis=1)
    kv[1, 0:ROWS, :] = mm(x_full, wqkv[:, COLS:]).astype(BF)
    kv_right = copies.remote(kv.at[1], kv.at[0], right)
    kv_left = copies.remote(kv.at[1], kv.at[2], left)

    first = lax.broadcasted_iota(jnp.int32, (ROWS, COLS), 1) < HEAD_DIM
    queries = mm(x_full, wqkv[:, 0:COLS])
    qm[0] = jnp.where(first, queries, 0.0).astype(BF)
    qm[1] = jnp.where(first, 0.0, queries).astype(BF)

    kv_right.wait_recv()
    kv_left.wait_recv()

    def reach(b, lo):
        return jnp.concatenate(
            [
                kv[e // 2, (e % 2) * BLOCK : (e % 2 + 1) * BLOCK, lo : lo + COLS]
                for e in range(b, b + REACH)
            ],
            axis=0,
        )

    live_ext = jnp.concatenate([kv[i, ROWS : ROWS + 16, :] for i in range(3)], axis=1)
    live_ext = live_ext.astype(F32)[0:1, :]
    first_b = first[0:BLOCK]
    span = REACH * BLOCK
    col = lax.broadcasted_iota(jnp.int32, (BLOCK, span), 1)
    row = lax.broadcasted_iota(jnp.int32, (BLOCK, span), 0)
    diag = col == row + 2 * BLOCK
    for b in range(2):
        rows = slice(b * BLOCK, (b + 1) * BLOCK)
        keys, vals = reach(b, 0), reach(b, COLS)
        block = lax.broadcasted_iota(jnp.int32, (1, span), 1) // BLOCK + (2 * node - 2 + b)
        chosen = (block == win_in[b, 0]) | (block == win_in[b, 1]) | (block == win_in[b, 2])
        usable = jnp.where(chosen, live_ext[:, b * BLOCK : b * BLOCK + span], 0.0)
        allowed = diag | (jnp.broadcast_to(usable, (BLOCK, span)) > 0.5)
        outs = []
        for h in range(2):
            scores = mm_nt(qm[h, rows, :], keys) * SCALE
            expo = jnp.where(allowed, jnp.exp(scores), 0.0)
            prob = expo / jnp.sum(expo, axis=-1, keepdims=True)
            probs[2 * b + h] = prob
            outs.append(mm(prob.astype(BF), vals))
        attn[rows, :] = jnp.where(first_b, outs[0], outs[1]).astype(BF)

    for copy in g_copies:
        copy.wait_recv()
    g_full = jnp.concatenate([gg[s] for s in range(SHARDS)], axis=1)
    back = mm_nt(g_full, wo[...])
    bm[0] = jnp.where(first, back, 0.0).astype(BF)
    bm[1] = jnp.where(first, 0.0, back).astype(BF)

    for b in range(2):
        rows = slice(b * BLOCK, (b + 1) * BLOCK)
        keys, vals = reach(b, 0), reach(b, COLS)
        outs, dk, dv = [], 0.0, 0.0
        for h in range(2):
            prob = probs[2 * b + h]
            dprob = mm_nt(bm[h, rows, :], vals)
            delta = jnp.sum(prob * dprob, axis=-1, keepdims=True)
            dscore = (SCALE * prob * (dprob - delta)).astype(BF)
            outs.append(mm(dscore, keys))
            dk = dk + mm_tn(dscore, qm[h, rows, :])
            dv = dv + mm_tn(prob.astype(BF), bm[h, rows, :])
        dq[rows, :] = jnp.where(first_b, outs[0], outs[1]).astype(BF)
        if b == 0:
            dkv_ext[0:span, 0:COLS] = dk
            dkv_ext[0:span, COLS:] = dv
        else:
            dkv_ext[BLOCK:span, 0:COLS] += dk[0 : span - BLOCK]
            dkv_ext[BLOCK:span, COLS:] += dv[0 : span - BLOCK]
            dkv_ext[span:, 0:COLS] = dk[span - BLOCK :]
            dkv_ext[span:, COLS:] = dv[span - BLOCK :]

    dkv_send[0] = dkv_ext[0:ROWS, :].astype(BF)
    dkv_send[1] = dkv_ext[2 * ROWS :, :].astype(BF)
    dkv_left = copies.remote(dkv_send.at[0], dkv_recv.at[0], left)
    dkv_right = copies.remote(dkv_send.at[1], dkv_recv.at[1], right)

    for s in range(SHARDS):
        terms[0, s] = mm_tn(xg[s], dq[...]).astype(BF)
        terms[1, s] = mm_tn(attn[...], gg[s]).astype(BF)
    core_copies = [copies.remote(terms.at[1 - core], core_recv.at[0], other)]

    dkv_left.wait_recv()
    dkv_right.wait_recv()
    dkv = dkv_ext[ROWS : 2 * ROWS, :] + dkv_recv[0].astype(F32) + dkv_recv[1].astype(F32)
    grads[:, 0:COLS] = dq[...]
    grads[:, COLS:] = dkv.astype(BF)
    for s in range(SHARDS):
        both = mm_tn(xg[s], grads[:, COLS:]).astype(BF)
        terms[2, s] = both[:, 0:COLS]
        terms[3, s] = both[:, COLS:]
    core_copies.append(copies.remote(terms.at[3 - core], core_recv.at[1], other))

    half, piece = BLOCK // 2, BLOCK // 8

    def low(i):
        return pl.ds(pl.multiple_of(i * piece, piece), piece)

    def high(i):
        return pl.ds(pl.multiple_of(half + i * piece, piece), piece)

    def first_reduce(e):
        core_copies[e].wait_recv()
        own = terms[2 * e + core].astype(F32) + core_recv[e].astype(F32)
        part[e] = own.astype(BF)
        a = [
            copies.remote(part.at[e, at_z(d), 0:half, :], ra1.at[e, d], z_dev(d))
            for d in range(1, NZ)
        ]
        b = [
            copies.remote(part.at[e, :, high(at_y(d)), :], rb1.at[e, d], y_dev(d))
            for d in range(1, NY)
        ]
        return a, b

    def second_reduce(e, a, b):
        for copy in a:
            copy.wait_recv()
        total = part[e, z, 0:half, :].astype(F32)
        for d in range(1, NZ):
            total = total + ra1[e, d].astype(F32)
        sa[e] = total.astype(BF)
        a = [copies.remote(sa.at[e, low(at_y(d)), :], ra2.at[e, d], y_dev(d)) for d in range(1, NY)]
        for copy in b:
            copy.wait_recv()
        total = part[e, :, high(y), :].astype(F32)
        for d in range(1, NY):
            total = total + rb1[e, d].astype(F32)
        sb[e] = total.astype(BF)
        b = [copies.remote(sb.at[e, at_z(d)], rb2.at[e, d], z_dev(d)) for d in range(1, NZ)]
        return a, b

    def first_gather(e, a, b):
        mine = 2 * e + core
        for copy in a:
            copy.wait_recv()
        total = sa[e, low(y), :].astype(F32)
        for d in range(1, NY):
            total = total + ra2[e, d].astype(F32)
        fin[mine, z, low(y), :] = total.astype(BF)
        ref = fin.at[mine, z, low(y), :]
        a = [copies.remote(ref, ref, y_dev(d)) for d in range(1, NY)]
        for copy in b:
            copy.wait_recv()
        total = sb[e, z].astype(F32)
        for d in range(1, NZ):
            total = total + rb2[e, d].astype(F32)
        fin[mine, z, high(y), :] = total.astype(BF)
        ref = fin.at[mine, z, high(y), :]
        b = [copies.remote(ref, ref, z_dev(d)) for d in range(1, NZ)]
        return a, b

    def second_gather(e, a, b):
        mine = 2 * e + core
        for copy in a:
            copy.wait_recv()
        ref = fin.at[mine, z, 0:half, :]
        a = [copies.remote(ref, ref, z_dev(d)) for d in range(1, NZ)]
        for copy in b:
            copy.wait_recv()
        ref = fin.at[mine, :, high(y), :]
        b = [copies.remote(ref, ref, y_dev(d)) for d in range(1, NY)]
        return a, b

    def last_gather(e, a, b):
        mine = 2 * e + core
        for copy in a + b:
            copy.wait_recv()
        ref = fin.at[mine]
        copy = copies.remote(ref, ref, other)
        out = pltpu.make_async_copy(ref, f_out.at[mine], out_sem.at[2 * e])
        out.start()
        return copy, out

    early = first_reduce(0)
    late = first_reduce(1)

    own_rows = pl.ds(pl.multiple_of(head * COLS, COLS), COLS)
    it_copies = []
    for d in range(1, SHARDS):
        rows = pl.ds(pl.multiple_of(at_head(d) * COLS, COLS), COLS)
        it_send[d] = mm_nt(grads[...], wqkv[rows, :]).astype(BF)
        it_copies.append(copies.remote(it_send.at[d], it_recv.at[d], head_dev(d)))

    early = second_reduce(0, *early)
    late = second_reduce(1, *late)
    early = first_gather(0, *early)
    late = first_gather(1, *late)

    total = mm_nt(grads[...], wqkv[own_rows, :])
    for copy in it_copies:
        copy.wait_recv()
    for d in range(1, SHARDS):
        total = total + it_recv[d].astype(F32)
    ig[...] = total.astype(BF)
    ig_copy = pltpu.make_async_copy(ig, ig_out, out_sem.at[4])
    ig_copy.start()

    early = second_gather(0, *early)
    late = second_gather(1, *late)
    early_copy, early_out = last_gather(0, *early)
    late_copy, late_out = last_gather(1, *late)
    early_copy.wait_recv()
    early_rest = pltpu.make_async_copy(fin.at[1 - core], f_out.at[1 - core], out_sem.at[1])
    early_rest.start()
    late_copy.wait_recv()
    late_rest = pltpu.make_async_copy(fin.at[3 - core], f_out.at[3 - core], out_sem.at[3])
    late_rest.start()
    for copy in copies.started:
        copy.wait_send()
    for out in (ig_copy, early_out, late_out, early_rest, late_rest):
        out.wait()


N_COPIES = 7 * 3 + 4 + 2 + 2 * 4 * (NZ - 1 + NY - 1) + 2


def body(inputs, out_grad, w_query, w_key, w_value, w_out, live_rows, window_blocks):
    anyspec = pl.BlockSpec(memory_space=pl.ANY)
    smem = pl.BlockSpec(memory_space=pltpu.SMEM)
    half, piece = BLOCK // 2, BLOCK // 8
    vm = pltpu.VMEM
    input_grad, fin = pl.pallas_call(
        kernel,
        out_shape=(
            jax.ShapeDtypeStruct((ROWS, COLS), BF),
            jax.ShapeDtypeStruct((4, SHARDS, BLOCK, COLS), BF),
        ),
        in_specs=[anyspec] * 6 + [smem] * 2,
        out_specs=(anyspec, anyspec),
        scratch_shapes=[
            vm((SHARDS, ROWS, COLS), BF),
            vm((SHARDS, ROWS, COLS), BF),
            vm((SHARDS * COLS, 3 * COLS), BF),
            vm((COLS, SHARDS * COLS), BF),
            vm((3, ROWS + 16, 2 * COLS), BF),
            vm((2, ROWS, COLS), BF),
            vm((2, ROWS, COLS), BF),
            vm((4, BLOCK, REACH * BLOCK), F32),
            vm((ROWS, COLS), BF),
            vm((ROWS, COLS), BF),
            vm((3 * ROWS, 2 * COLS), F32),
            vm((2, ROWS, 2 * COLS), BF),
            vm((2, ROWS, 2 * COLS), BF),
            vm((ROWS, 3 * COLS), BF),
            vm((4, SHARDS, BLOCK, COLS), BF),
            vm((2, SHARDS, BLOCK, COLS), BF),
            vm((2, SHARDS, BLOCK, COLS), BF),
            vm((2, NZ, half, COLS), BF),
            vm((2, NY, SHARDS, piece, COLS), BF),
            vm((2, half, COLS), BF),
            vm((2, SHARDS, piece, COLS), BF),
            vm((2, NY, piece, COLS), BF),
            vm((2, NZ, piece, COLS), BF),
            vm((4, SHARDS, BLOCK, COLS), BF),
            vm((SHARDS, ROWS, COLS), BF),
            vm((SHARDS, ROWS, COLS), BF),
            vm((ROWS, COLS), BF),
            pltpu.SemaphoreType.DMA((6,)),
            pltpu.SemaphoreType.DMA((N_COPIES,)),
            pltpu.SemaphoreType.DMA((N_COPIES,)),
            pltpu.SemaphoreType.DMA((5,)),
        ],
        compiler_params=pltpu.CompilerParams(
            collective_id=0, has_side_effects=True, vmem_limit_bytes=40 * 1024 * 1024
        ),
        cost_estimate=pl.CostEstimate(
            flops=1200000000, bytes_accessed=3000000, transcendentals=400000
        ),
    )(inputs, out_grad, w_query, w_key, w_value, w_out, live_rows, window_blocks)
    width = SHARDS * COLS
    grad_query = fin[0].reshape(width, COLS)
    grad_out = fin[1].transpose(1, 0, 2).reshape(COLS, width)
    grad_key = fin[2].reshape(width, COLS)
    grad_value = fin[3].reshape(width, COLS)
    return (input_grad, grad_query, grad_key, grad_value, grad_out)


def solution(mesh):
    placed = (
        P("nodes", "heads"),
        P("nodes", "heads"),
        P(None, "heads"),
        P(None, "heads"),
        P(None, "heads"),
        P("heads", None),
        P("nodes"),
        P("nodes", None),
    )
    return jax.shard_map(
        body,
        mesh=mesh,
        in_specs=placed,
        out_specs=(
            P("nodes", "heads"),
            P(None, "heads"),
            P(None, "heads"),
            P(None, "heads"),
            P("heads", None),
        ),
        check_vma=False,
    )
```

time: 430 us -> 83.1 us (0.19)
  the two profiles are of different devices: /device:TPU:32 before, /device:TPU:1 now
where the time goes in v1:
time: 83.1 us; the launch traced here: 82.8 us
  Pallas kernels  73.4 us (88%)
  local copies, waits for them, and re-layouts  8.04 us (10%)
  between operations  1.33 us (2%)
    pallas_call x1, Pallas kernels, body(): pl.pallas_call(kernel, out_shape=(jax.ShapeDtypeStruct((ROWS, COLS), BF),...  73.4 us
    unnamed x16, local copies, waits for them, and re-layouts  6.97 us

profile of v1, /device:TPU:1, one launch (start us, length us, event | category | flops | bytes accessed | tf_op | source)
XLA Modules:
  0.0 82.8 jit_solution(12479521437144525632)
XLA Ops:
  0.6 0.0 copy-start.6
  1.3 0.0 copy-done.6
  1.3 0.0 copy-start
  1.3 0.9 %copy-done = bf16[1024,128]{1,0:T(8,128)(2,1)S(1)} copy-done((bf16[1024,128]{1,0:T(8,128)(2,1)S(1)}, bf16[1024,128]{1,0:T(8,128)(2,1)}, u32[]{:S(2)}) %copy-start) | copy-done | bytes 262168
  2.3 0.0 copy-start.1
  2.3 0.9 %copy-done.1 = bf16[1024,128]{1,0:T(8,128)(2,1)S(1)} copy-done((bf16[1024,128]{1,0:T(8,128)(2,1)S(1)}, bf16[1024,128]{1,0:T(8,128)(2,1)}, u32[]{:S(2)}) %copy-start.1) | copy-done | bytes 262168
  3.2 0.0 copy-start.2
  3.2 0.9 %copy-done.2 = bf16[1024,128]{1,0:T(8,128)(2,1)S(1)} copy-done((bf16[1024,128]{1,0:T(8,128)(2,1)S(1)}, bf16[1024,128]{1,0:T(8,128)(2,1)}, u32[]{:S(2)}) %copy-start.2) | copy-done | bytes 262168
  4.2 0.0 copy-start.3
  4.2 0.9 %copy-done.3 = bf16[128,1024]{1,0:T(8,128)(2,1)S(1)} copy-done((bf16[128,1024]{1,0:T(8,128)(2,1)S(1)}, bf16[128,1024]{1,0:T(8,128)(2,1)}, u32[]{:S(2)}) %copy-start.3) | copy-done | bytes 262168
  5.1 0.0 copy-start.4
  5.1 0.8 %copy-done.4 = bf16[256,128]{1,0:T(8,128)(2,1)S(1)} copy-done((bf16[256,128]{1,0:T(8,128)(2,1)S(1)}, bf16[256,128]{1,0:T(8,128)(2,1)}, u32[]{:S(2)}) %copy-start.4) | copy-done | bytes 65560
  6.0 0.0 copy-start.5
  6.0 0.8 %copy-done.5 = bf16[256,128]{1,0:T(8,128)(2,1)S(1)} copy-done((bf16[256,128]{1,0:T(8,128)(2,1)S(1)}, bf16[256,128]{1,0:T(8,128)(2,1)}, u32[]{:S(2)}) %copy-start.5) | copy-done | bytes 65560
  6.8 73.4 %shard_map.119 = (bf16[256,128]{1,0:T(8,128)(2,1)S(1)}, bf16[4,8,128,128]{3,2,1,0:T(8,128)(2,1)S(1)}) custom-call(bf16[256,128]{1,0:T(8,128)(2,1)S(1)} %copy-done.4, bf16[256,128]{1,0:T(8,128)(2,1)S(1)} %copy-done.5, bf16[1024,128]{1,0:T(8,128)(2,1)S(1)} %copy-done, bf16[1024,128]{1,0:T(8,128)(2,1)S(1)} %copy-done.1, bf16[1024,128]{1,0:T(8,128)(2,1)S(1)} %copy-done.2, ...), custom_call_target="tpu_custom_call" | custom-call | flops 1200000000 | bytes 3000000 | tf_op jit(solution)/shard_map/pallas_call | solution.py:351
  80.2 0.9 %slice_bitcast_fusion = (bf16[128,8,128]{2,0,1:T(8,128)(2,1)S(1)}, bf16[1,8,128,128]{3,2,1,0:T(8,128)(2,1)}, bf16[1,8,128,128]{3,2,1,0:T(8,128)(2,1)}, bf16[1,8,128,128]{3,2,1,0:T(8,128)(2,1)}) fusion(bf16[4,8,128,128]{3,2,1,0:T(8,128)(2,1)S(1)} %get-tuple-element.8), kind=kLoop, calls=%fused_computation | loop fusion | bytes 2097152 | tf_op jit(solution)/shard_map/transpose | solution.py:401
  81.1 0.2 copy.13
  81.3 0.9 %copy.14 = bf16[128,1024]{1,0:T(8,128)(2,1)} copy(bf16[128,1024]{0,1:T(8,128)(2,1)S(1)} %bitcast.8) | data formatting | bytes 524288
  82.2 0.6 copy.17
Async XLA Ops:
  0.6 0.7 copy-start.6
  1.3 0.9 %copy-start = (bf16[1024,128]{1,0:T(8,128)(2,1)S(1)}, bf16[1024,128]{1,0:T(8,128)(2,1)}, u32[]{:S(2)}) copy-start(bf16[1024,128]{1,0:T(8,128)(2,1)} %wq_in.1) | copy-start | bytes 786436
  2.3 0.9 %copy-start.1 = (bf16[1024,128]{1,0:T(8,128)(2,1)S(1)}, bf16[1024,128]{1,0:T(8,128)(2,1)}, u32[]{:S(2)}) copy-start(bf16[1024,128]{1,0:T(8,128)(2,1)} %wk_in.1) | copy-start | bytes 786436
  3.2 0.9 %copy-start.2 = (bf16[1024,128]{1,0:T(8,128)(2,1)S(1)}, bf16[1024,128]{1,0:T(8,128)(2,1)}, u32[]{:S(2)}) copy-start(bf16[1024,128]{1,0:T(8,128)(2,1)} %wv_in.1) | copy-start | bytes 786436
  4.2 0.9 %copy-start.3 = (bf16[128,1024]{1,0:T(8,128)(2,1)S(1)}, bf16[128,1024]{1,0:T(8,128)(2,1)}, u32[]{:S(2)}) copy-start(bf16[128,1024]{1,0:T(8,128)(2,1)} %wo_in.1) | copy-start | bytes 786436
  5.1 0.8 %copy-start.4 = (bf16[256,128]{1,0:T(8,128)(2,1)S(1)}, bf16[256,128]{1,0:T(8,128)(2,1)}, u32[]{:S(2)}) copy-start(bf16[256,128]{1,0:T(8,128)(2,1)} %x_in.1) | copy-start | bytes 196612
  6.0 0.8 %copy-start.5 = (bf16[256,128]{1,0:T(8,128)(2,1)S(1)}, bf16[256,128]{1,0:T(8,128)(2,1)}, u32[]{:S(2)}) copy-start(bf16[256,128]{1,0:T(8,128)(2,1)} %g_in.1) | copy-start | bytes 196612

commit v2 on v1

v2 whole, which is shorter than its diff:
```python
import functools

import jax
import jax.numpy as jnp
from jax import lax
from jax.experimental import pallas as pl
from jax.experimental.pallas import tpu as pltpu
from jax.sharding import PartitionSpec as P

HEAD_DIM = 64
BLOCK = 128
REACH = 5
ROWS = 256
COLS = 128
SHARDS = 8
NZ = 8
NY = 4
NX = 4
SCALE = HEAD_DIM ** (-0.5)
BF = jnp.bfloat16
F32 = jnp.float32
MESH = pl.DeviceIdType.MESH
NT = (((1,), (1,)), ((), ()))
TN = (((0,), (0,)), ((), ()))


def mm(a, b):
    return jnp.dot(a, b, preferred_element_type=F32)


def mm_nt(a, b):
    return lax.dot_general(a, b, NT, preferred_element_type=F32)


def mm_tn(a, b):
    return lax.dot_general(a, b, TN, preferred_element_type=F32)


class Copies:
    def __init__(self, send, recv):
        self.send, self.recv, self.used, self.started = send, recv, 0, []

    def planned(self, src, dst, device):
        i = self.used
        self.used += 1
        return pltpu.make_async_remote_copy(
            src_ref=src,
            dst_ref=dst,
            send_sem=self.send.at[i],
            recv_sem=self.recv.at[i],
            device_id=device,
            device_id_type=MESH,
        )

    def remote(self, src, dst, device):
        copy = self.planned(src, dst, device)
        copy.start()
        self.started.append(copy)
        return copy


def kernel(
    x_in, g_in, wq_in, wk_in, wv_in, wo_in, live_in, win_in,
    ig_out, f_out,
    xg, gg, xo, go, xt, wqkv, wqkv_t, wo, wo_t, kv, qm, bm, probs, ad, ad_other, late_other,
    dkv_ext, dkv_send, dkv_recv, grads,
    part, ra1, rb1, sa, sb, ra2, rb2, fin, it_send, it_recv, it_pass, it_last, ig,
    local_sem, send_sem, recv_sem, out_sem,
):
    node = lax.axis_index("nodes")
    head = lax.axis_index("heads")
    core = lax.rem(node, 2)
    z = lax.rem(node // 2, NZ)
    y = node // (2 * NZ)
    nodes = 2 * NZ * NY
    xx = head // 2
    yl = lax.rem(head, 2)

    def at_z(d):
        return lax.rem(z + d, NZ)

    def at_y(d):
        return lax.rem(y + d, NY)

    def at_x(d):
        return lax.rem(xx + d, NX)

    left = (lax.rem(node + nodes - 1, nodes), head)
    right = (lax.rem(node + 1, nodes), head)
    other = (node + 1 - 2 * core, head)

    def z_dev(d):
        return ((y * NZ + at_z(d)) * 2 + core, head)

    def y_dev(d):
        return ((at_y(d) * NZ + z) * 2 + core, head)

    def x_dev(d):
        return (node, at_x(d) * 2 + yl)

    mate_head = xx * 2 + 1 - yl
    mate = (node, mate_head)

    partners = [mate]
    partners += [x_dev(d) for d in range(1, NX)]
    partners += [left, right]
    partners += [z_dev(d) for d in range(1, NZ)]
    partners += [y_dev(d) for d in range(1, NY)]
    barrier = pltpu.get_barrier_semaphore()
    for dev in partners:
        pl.semaphore_signal(barrier, inc=1, device_id=dev, device_id_type=MESH)

    loads = [
        pltpu.make_async_copy(x_in, xg.at[head], local_sem.at[0]),
        pltpu.make_async_copy(wq_in, wqkv.at[0], local_sem.at[1]),
        pltpu.make_async_copy(wk_in, wqkv.at[1], local_sem.at[2]),
        pltpu.make_async_copy(wv_in, wqkv.at[2], local_sem.at[3]),
        pltpu.make_async_copy(g_in, gg.at[head], local_sem.at[4]),
        pltpu.make_async_copy(wo_in, wo, local_sem.at[5]),
    ]
    for load in loads:
        load.start()

    pl.semaphore_wait(barrier, len(partners))
    copies = Copies(send_sem, recv_sem)
    x_a = copies.remote(x_in, xg.at[head], mate)
    x_b = {d: copies.remote(x_in, xg.at[head], x_dev(d)) for d in (1, 3, 2)}
    g_a = copies.remote(g_in, gg.at[head], mate)

    live = live_in[0]
    lane_row = lax.broadcasted_iota(jnp.int32, (16, ROWS), 1)
    kv[1, ROWS : ROWS + 16, :] = jnp.where(lane_row < live, 1.0, 0.0).astype(BF)
    for load in loads:
        load.wait()

    x_a.wait_recv()
    x_c = [copies.remote(xg.at[mate_head], xg.at[mate_head], x_dev(d)) for d in (1, 3)]
    g_b = {d: copies.remote(g_in, gg.at[head], x_dev(d)) for d in (1, 3, 2)}
    far = at_x(2) * 2 + yl
    for j in range(3):
        for s in range(SHARDS):
            wqkv_t[s, j * COLS : (j + 1) * COLS, :] = wqkv[j, s * COLS : (s + 1) * COLS, :].T
    x_b[2].wait_recv()
    x_d = copies.remote(xg.at[far], xg.at[far], mate)
    g_a.wait_recv()
    g_c = [copies.remote(gg.at[mate_head], gg.at[mate_head], x_dev(d)) for d in (1, 3)]
    for copy in (x_b[1], x_b[3], x_c[0], x_c[1], x_d):
        copy.wait_recv()

    x_full = jnp.concatenate([xg[s] for s in range(SHARDS)], axis=1)
    kv[1, 0:ROWS, 0:COLS] = mm(x_full, wqkv[1]).astype(BF)
    kv[1, 0:ROWS, COLS:] = mm(x_full, wqkv[2]).astype(BF)
    kv_right = copies.remote(kv.at[1], kv.at[0], right)
    kv_left = copies.remote(kv.at[1], kv.at[2], left)
    x_core = copies.remote(xg, xo, other)

    first = lax.broadcasted_iota(jnp.int32, (ROWS, COLS), 1) < HEAD_DIM
    queries = mm(x_full, wqkv[0])
    qm[0] = jnp.where(first, queries, 0.0).astype(BF)
    qm[1] = jnp.where(first, 0.0, queries).astype(BF)
    g_b[2].wait_recv()
    g_d = copies.remote(gg.at[far], gg.at[far], mate)
    for s in range(SHARDS):
        xt[s, :, 0:ROWS] = xg[s].T
    for s in range(SHARDS):
        wo_t[s * COLS : (s + 1) * COLS, :] = wo[:, s * COLS : (s + 1) * COLS].T

    kv_right.wait_recv()
    kv_left.wait_recv()

    def reach(b, lo):
        return jnp.concatenate(
            [
                kv[e // 2, (e % 2) * BLOCK : (e % 2 + 1) * BLOCK, lo : lo + COLS]
                for e in range(b, b + REACH)
            ],
            axis=0,
        )

    live_ext = jnp.concatenate([kv[i, ROWS : ROWS + 16, :] for i in range(3)], axis=1)
    live_ext = live_ext.astype(F32)[0:1, :]
    first_b = first[0:BLOCK]
    span = REACH * BLOCK
    col = lax.broadcasted_iota(jnp.int32, (BLOCK, span), 1)
    row = lax.broadcasted_iota(jnp.int32, (BLOCK, span), 0)
    diag = col == row + 2 * BLOCK
    for b in range(2):
        rows = slice(b * BLOCK, (b + 1) * BLOCK)
        keys, vals = reach(b, 0), reach(b, COLS)
        block = lax.broadcasted_iota(jnp.int32, (1, span), 1) // BLOCK + (2 * node - 2 + b)
        chosen = (block == win_in[b, 0]) | (block == win_in[b, 1]) | (block == win_in[b, 2])
        usable = jnp.where(chosen, live_ext[:, b * BLOCK : b * BLOCK + span], 0.0)
        allowed = diag | (jnp.broadcast_to(usable, (BLOCK, span)) > 0.5)
        outs = []
        for h in range(2):
            scores = mm_nt(qm[h, rows, :], keys) * SCALE
            expo = jnp.where(allowed, jnp.exp(scores), 0.0)
            prob = expo / jnp.sum(expo, axis=-1, keepdims=True)
            probs[2 * b + h] = prob
            outs.append(mm(prob.astype(BF), vals))
        ad[1, rows, :] = jnp.where(first_b, outs[0], outs[1]).astype(BF)

    early_copy = copies.planned(ad.at[1 - core], ad_other, other)

    @pl.when(core == 0)
    def _():
        early_copy.start()

    x_core.wait_recv()
    for s in range(SHARDS):
        xt[s, :, ROWS:] = xo[s].T

    for copy in (g_b[1], g_b[3], g_c[0], g_c[1], g_d):
        copy.wait_recv()
    g_core = copies.planned(gg, go, other)

    @pl.when(core == 0)
    def _():
        g_core.start()

    g_full = jnp.concatenate([gg[s] for s in range(SHARDS)], axis=1)
    back = mm(g_full, wo_t[...])
    bm[0] = jnp.where(first, back, 0.0).astype(BF)
    bm[1] = jnp.where(first, 0.0, back).astype(BF)

    for b in range(2):
        rows = slice(b * BLOCK, (b + 1) * BLOCK)
        keys, vals = reach(b, 0), reach(b, COLS)
        outs, dk, dv = [], 0.0, 0.0
        for h in range(2):
            prob = probs[2 * b + h]
            dprob = mm_nt(bm[h, rows, :], vals)
            delta = jnp.sum(prob * dprob, axis=-1, keepdims=True)
            dscore = (SCALE * prob * (dprob - delta)).astype(BF)
            outs.append(mm(dscore, keys))
            dk = dk + mm_tn(dscore, qm[h, rows, :])
            dv = dv + mm_tn(prob.astype(BF), bm[h, rows, :])
        ad[0, rows, :] = jnp.where(first_b, outs[0], outs[1]).astype(BF)
        if b == 0:
            dkv_ext[0:span, 0:COLS] = dk
            dkv_ext[0:span, COLS:] = dv
        else:
            dkv_ext[BLOCK:span, 0:COLS] += dk[0 : span - BLOCK]
            dkv_ext[BLOCK:span, COLS:] += dv[0 : span - BLOCK]
            dkv_ext[span:, 0:COLS] = dk[span - BLOCK :]
            dkv_ext[span:, COLS:] = dv[span - BLOCK :]

    dkv_send[0] = dkv_ext[0:ROWS, :].astype(BF)
    dkv_send[1] = dkv_ext[2 * ROWS :, :].astype(BF)
    dkv_left = copies.remote(dkv_send.at[0], dkv_recv.at[0], left)
    dkv_right = copies.remote(dkv_send.at[1], dkv_recv.at[1], right)

    @pl.when(core == 1)
    def _():
        early_copy.start()


    half, piece = BLOCK // 2, BLOCK // 8

    def low(i):
        return pl.ds(pl.multiple_of(i * piece, piece), piece)

    def high(i):
        return pl.ds(pl.multiple_of(half + i * piece, piece), piece)

    def first_reduce(e):
        a = [
            copies.remote(part.at[e, at_z(d), 0:half, :], ra1.at[e, d], z_dev(d))
            for d in range(1, NZ)
        ]
        b = [
            copies.remote(part.at[e, :, high(at_y(d)), :], rb1.at[e, d], y_dev(d))
            for d in range(1, NY)
        ]
        return a, b

    def second_reduce(e, a, b):
        for copy in a:
            copy.wait_recv()
        total = part[e, z, 0:half, :].astype(F32)
        for d in range(1, NZ):
            total = total + ra1[e, d].astype(F32)
        sa[e] = total.astype(BF)
        a = [copies.remote(sa.at[e, low(at_y(d)), :], ra2.at[e, d], y_dev(d)) for d in range(1, NY)]
        for copy in b:
            copy.wait_recv()
        total = part[e, :, high(y), :].astype(F32)
        for d in range(1, NY):
            total = total + rb1[e, d].astype(F32)
        sb[e] = total.astype(BF)
        b = [copies.remote(sb.at[e, at_z(d)], rb2.at[e, d], z_dev(d)) for d in range(1, NZ)]
        return a, b

    def first_gather(e, a, b):
        mine = 2 * e + core
        for copy in a:
            copy.wait_recv()
        total = sa[e, low(y), :].astype(F32)
        for d in range(1, NY):
            total = total + ra2[e, d].astype(F32)
        fin[e, z, low(y), :] = total.astype(BF)
        ref = fin.at[e, z, low(y), :]
        a = [copies.remote(ref, ref, y_dev(d)) for d in range(1, NY)]
        for copy in b:
            copy.wait_recv()
        total = sb[e, z].astype(F32)
        for d in range(1, NZ):
            total = total + rb2[e, d].astype(F32)
        fin[e, z, high(y), :] = total.astype(BF)
        ref = fin.at[e, z, high(y), :]
        b = [copies.remote(ref, ref, z_dev(d)) for d in range(1, NZ)]
        return a, b

    def second_gather(e, a, b):
        for copy in a:
            copy.wait_recv()
        ref = fin.at[e, z, 0:half, :]
        a = [copies.remote(ref, ref, z_dev(d)) for d in range(1, NZ)]
        for copy in b:
            copy.wait_recv()
        ref = fin.at[e, :, high(y), :]
        b = [copies.remote(ref, ref, y_dev(d)) for d in range(1, NY)]
        return a, b

    def last_gather(e, a, b, whole):
        mine = 2 * e + core
        handed = []
        if not whole:
            handed.append(
                copies.remote(fin.at[e, z, 0:half, :], f_out.at[mine, z, 0:half, :], other)
            )
            handed.append(
                copies.remote(fin.at[e, :, high(y), :], f_out.at[mine, :, high(y), :], other)
            )
        for d, copy in zip(range(1, NZ), a):
            copy.wait_recv()
            if not whole:
                at = at_z(NZ - d)
                handed.append(
                    copies.remote(fin.at[e, at, 0:half, :], f_out.at[mine, at, 0:half, :], other)
                )
        for d, copy in zip(range(1, NY), b):
            copy.wait_recv()
            if not whole:
                at = high(at_y(NY - d))
                handed.append(
                    copies.remote(fin.at[e, :, at, :], f_out.at[mine, :, at, :], other)
                )
        if whole:
            handed.append(copies.remote(fin.at[e], f_out.at[mine], other))
        out = pltpu.make_async_copy(fin.at[e], f_out.at[mine], out_sem.at[e])
        out.start()
        return handed, out

    early_copy.wait_recv()

    @pl.when(core == 0)
    def _():
        part[0, :, :, :] = (
            mm(
                xt[...].reshape(SHARDS * COLS, 2 * ROWS),
                jnp.concatenate([ad[0], ad_other[...]], axis=0),
            )
            .astype(BF)
            .reshape(SHARDS, COLS, COLS)
        )

    @pl.when(core == 1)
    def _():
        g_core.wait_recv()
        lhs = jnp.concatenate([ad[1].T, ad_other[...].T], axis=1)
        for s in range(SHARDS):
            part[0, s] = mm(lhs, jnp.concatenate([gg[s], go[s]], axis=0)).astype(BF)

    early = first_reduce(0)
    dkv_left.wait_recv()
    dkv_right.wait_recv()
    dkv = dkv_ext[ROWS : 2 * ROWS, :] + dkv_recv[0].astype(F32) + dkv_recv[1].astype(F32)
    grads[0] = dkv[:, 0:COLS].astype(BF)
    grads[1] = dkv[:, COLS:].astype(BF)
    late_copy = copies.remote(grads.at[1 - core], late_other, other)

    all_grads = jnp.concatenate([ad[0], grads[0], grads[1]], axis=1)
    it_copies = []
    for d in range(1, NX):
        for i in range(2):
            it_send[d, i] = mm(all_grads, wqkv_t[at_x(d) * 2 + i]).astype(BF)
        it_copies.append(copies.remote(it_send.at[d], it_recv.at[d], x_dev(d)))

    late_copy.wait_recv()
    part[1, :, :, :] = (
        mm(
            xt[...].reshape(SHARDS * COLS, 2 * ROWS),
            jnp.concatenate([grads[core], late_other[...]], axis=0),
        )
        .astype(BF)
        .reshape(SHARDS, COLS, COLS)
    )
    late = first_reduce(1)

    it_keep = mm(all_grads, wqkv_t[head])
    it_give = mm(all_grads, wqkv_t[mate_head])

    early = second_reduce(0, *early)
    for copy in it_copies:
        copy.wait_recv()
    for d in range(1, NX):
        it_keep = it_keep + it_recv[d, yl].astype(F32)
        it_give = it_give + it_recv[d, 1 - yl].astype(F32)
    it_pass[...] = it_give.astype(BF)
    it_copy = copies.remote(it_pass, it_last, mate)
    late = second_reduce(1, *late)
    early = first_gather(0, *early)
    late = first_gather(1, *late)

    it_copy.wait_recv()
    ig[...] = (it_keep + it_last[...].astype(F32)).astype(BF)
    ig_copy = pltpu.make_async_copy(ig, ig_out, out_sem.at[2])
    ig_copy.start()

    early = second_gather(0, *early)
    late = second_gather(1, *late)
    early_handed, early_out = last_gather(0, *early, True)
    late_handed, late_out = last_gather(1, *late, False)
    for copy in early_handed + late_handed:
        copy.wait_recv()
    for copy in copies.started:
        copy.wait_send()

    @pl.when(core == 0)
    def _():
        early_copy.wait_send()
        g_core.wait_send()

    @pl.when(core == 1)
    def _():
        early_copy.wait_send()

    for out in (ig_copy, early_out, late_out):
        out.wait()


N_COPIES = 14 + 4 + 4 + 4 + 2 * 4 * (NZ - 1 + NY - 1) + 1 + NZ + NY


def hand_out(ig_in, f_in, ig_out, q_out, k_out, v_out, o_out, sem):
    parts = [(ig_in, ig_out), (f_in.at[0], q_out), (f_in.at[2], k_out), (f_in.at[3], v_out)]
    parts += [(f_in.at[1, s], o_out.at[:, s * COLS : (s + 1) * COLS]) for s in range(SHARDS)]
    copies = [pltpu.make_async_copy(a, b, sem.at[i]) for i, (a, b) in enumerate(parts)]
    for copy in copies:
        copy.start()
    for copy in copies:
        copy.wait()


def body(inputs, out_grad, w_query, w_key, w_value, w_out, live_rows, window_blocks):
    anyspec = pl.BlockSpec(memory_space=pl.ANY)
    smem = pl.BlockSpec(memory_space=pltpu.SMEM)
    half, piece = BLOCK // 2, BLOCK // 8
    vm = pltpu.VMEM
    params = pltpu.CompilerParams(
        collective_id=0, has_side_effects=True, vmem_limit_bytes=62 * 1024 * 1024
    )
    input_grad, fin = pl.pallas_call(
        kernel,
        out_shape=(
            jax.ShapeDtypeStruct((ROWS, COLS), BF),
            jax.ShapeDtypeStruct((4, SHARDS, BLOCK, COLS), BF),
        ),
        in_specs=[anyspec] * 6 + [smem] * 2,
        out_specs=(anyspec, anyspec),
        scratch_shapes=[
            vm((SHARDS, ROWS, COLS), BF),
            vm((SHARDS, ROWS, COLS), BF),
            vm((SHARDS, ROWS, COLS), BF),
            vm((SHARDS, ROWS, COLS), BF),
            vm((SHARDS, COLS, 2 * ROWS), BF),
            vm((3, SHARDS * COLS, COLS), BF),
            vm((SHARDS, 3 * COLS, COLS), BF),
            vm((COLS, SHARDS * COLS), BF),
            vm((SHARDS * COLS, COLS), BF),
            vm((3, ROWS + 16, 2 * COLS), BF),
            vm((2, ROWS, COLS), BF),
            vm((2, ROWS, COLS), BF),
            vm((4, BLOCK, REACH * BLOCK), F32),
            vm((2, ROWS, COLS), BF),
            vm((ROWS, COLS), BF),
            vm((ROWS, COLS), BF),
            vm((3 * ROWS, 2 * COLS), F32),
            vm((2, ROWS, 2 * COLS), BF),
            vm((2, ROWS, 2 * COLS), BF),
            vm((2, ROWS, COLS), BF),
            vm((2, SHARDS, BLOCK, COLS), BF),
            vm((2, NZ, half, COLS), BF),
            vm((2, NY, SHARDS, piece, COLS), BF),
            vm((2, half, COLS), BF),
            vm((2, SHARDS, piece, COLS), BF),
            vm((2, NY, piece, COLS), BF),
            vm((2, NZ, piece, COLS), BF),
            vm((2, SHARDS, BLOCK, COLS), BF),
            vm((NX, 2, ROWS, COLS), BF),
            vm((NX, 2, ROWS, COLS), BF),
            vm((ROWS, COLS), BF),
            vm((ROWS, COLS), BF),
            vm((ROWS, COLS), BF),
            pltpu.SemaphoreType.DMA((6,)),
            pltpu.SemaphoreType.DMA((N_COPIES,)),
            pltpu.SemaphoreType.DMA((N_COPIES,)),
            pltpu.SemaphoreType.DMA((3,)),
        ],
        compiler_params=params,
        cost_estimate=pl.CostEstimate(
            flops=1200000000, bytes_accessed=3000000, transcendentals=400000
        ),
    )(inputs, out_grad, w_query, w_key, w_value, w_out, live_rows, window_blocks)
    width = SHARDS * COLS
    cols = jax.ShapeDtypeStruct((SHARDS, COLS, COLS), BF)
    input_grad, grad_query, grad_key, grad_value, grad_out = pl.pallas_call(
        hand_out,
        out_shape=(
            jax.ShapeDtypeStruct((ROWS, COLS), BF),
            cols,
            cols,
            cols,
            jax.ShapeDtypeStruct((COLS, width), BF),
        ),
        in_specs=[anyspec] * 2,
        out_specs=[anyspec] * 5,
        scratch_shapes=[pltpu.SemaphoreType.DMA((4 + SHARDS,))],
        cost_estimate=pl.CostEstimate(flops=0, bytes_accessed=2200000, transcendentals=0),
    )(input_grad, fin)
    return (
        input_grad,
        grad_query.reshape(width, COLS),
        grad_key.reshape(width, COLS),
        grad_value.reshape(width, COLS),
        grad_out,
    )


def solution(mesh):
    placed = (
        P("nodes", "heads"),
        P("nodes", "heads"),
        P(None, "heads"),
        P(None, "heads"),
        P(None, "heads"),
        P("heads", None),
        P("nodes"),
        P("nodes", None),
    )
    return jax.shard_map(
        body,
        mesh=mesh,
        in_specs=placed,
        out_specs=(
            P("nodes", "heads"),
            P(None, "heads"),
            P(None, "heads"),
            P(None, "heads"),
            P("heads", None),
        ),
        check_vma=False,
    )
```

time: 83.1 us -> 107 us (1.29)
  the two profiles are of different devices: /device:TPU:1 before, /device:TPU:9 now
where the time goes in v2:
time: 107 us
  Pallas kernels  106 us (99%)
  between operations  1.29 us (1%)
    pallas_call x1, Pallas kernels, body(): pl.pallas_call(kernel, out_shape=(jax.ShapeDtypeStruct((ROWS, COLS), BF),...  70.6 us
    pallas_call x1, Pallas kernels, body(): pl.pallas_call(hand_out, out_shape=(jax.ShapeDtypeStruct((ROWS, COLS), BF...  35 us

profile of v2, /device:TPU:9, one launch (start us, length us, event | category | flops | bytes accessed | tf_op | source)
XLA Modules:
  0.0 106.9 jit_solution(7603512709703729146)
XLA Ops:
  1.3 70.6 %shard_map.119 = (bf16[256,128]{1,0:T(8,128)(2,1)}, bf16[4,8,128,128]{3,2,1,0:T(8,128)(2,1)}) custom-call(bf16[256,128]{1,0:T(8,128)(2,1)} %x_in.1, bf16[256,128]{1,0:T(8,128)(2,1)} %g_in.1, bf16[1024,128]{1,0:T(8,128)(2,1)} %wq_in.1, bf16[1024,128]{1,0:T(8,128)(2,1)} %wk_in.1, bf16[1024,128]{1,0:T(8,128)(2,1)} %wv_in.1, bf16[128,1024]{1,0:T(8,128)(2,1)} %wo_in.1, ...), custom_call_target="tpu_custom_call" | custom-call | flops 1200000000 | bytes 3000000 | tf_op jit(solution)/shard_map/pallas_call | solution.py:464
  71.9 35.0 %shard_map.120 = (bf16[256,128]{1,0:T(8,128)(2,1)}, bf16[8,128,128]{2,1,0:T(8,128)(2,1)}, bf16[8,128,128]{2,1,0:T(8,128)(2,1)}, bf16[8,128,128]{2,1,0:T(8,128)(2,1)}, bf16[128,1024]{1,0:T(8,128)(2,1)}) custom-call(bf16[256,128]{1,0:T(8,128)(2,1)} %get-tuple-element.12.ig_in, bf16[4,8,128,128]{3,2,1,0:T(8,128)(2,1)} %get-tuple-element.13.f_in), custom_call_target="tpu_custom_call" | custom-call | bytes 2200000 | tf_op jit(solution)/shard_map/pallas_call | solution.py:518

commit v3 on v2

v3 whole, which is shorter than its diff:
```python
import functools

import jax
import jax.numpy as jnp
from jax import lax
from jax.experimental import pallas as pl
from jax.experimental.pallas import tpu as pltpu
from jax.sharding import PartitionSpec as P

HEAD_DIM = 64
BLOCK = 128
ROWS = 256
COLS = 128
SHARDS = 8
NZ = 8
NY = 4
NX = 4
Z_ORDER = (4, 3, 5, 2, 6, 1, 7)
Y_ORDER = (2, 1, 3)
X_ORDER = (2, 1, 3)
TOP = 80
SCALE = HEAD_DIM ** (-0.5)
BF = jnp.bfloat16
F32 = jnp.float32
MESH = pl.DeviceIdType.MESH
NT = (((1,), (1,)), ((), ()))
TN = (((0,), (0,)), ((), ()))


def mm(a, b):
    return jnp.dot(a, b, preferred_element_type=F32)


def mm_nt(a, b):
    return lax.dot_general(a, b, NT, preferred_element_type=F32)


def mm_tn(a, b):
    return lax.dot_general(a, b, TN, preferred_element_type=F32)


class Copies:
    def __init__(self, send, recv):
        self.send, self.recv, self.used, self.started = send, recv, 0, []

    def planned(self, src, dst, device):
        i = self.used
        self.used += 1
        return pltpu.make_async_remote_copy(
            src_ref=src,
            dst_ref=dst,
            send_sem=self.send.at[i],
            recv_sem=self.recv.at[i],
            device_id=device,
            device_id_type=MESH,
        )

    def remote(self, src, dst, device):
        copy = self.planned(src, dst, device)
        copy.start()
        self.started.append(copy)
        return copy


def kernel(
    x_in, g_in, wq_in, wk_in, wv_in, wo_in, live_in, win_in,
    ig_out, f_out,
    xg, gg, xo, go, xt, wq, wkv, w_t, wo, wo_t, kv, qs, bs, expo, dprob, ad, ad_other, late_other,
    dkv_own, dkv_send, dkv_recv, grads,
    part, ra1, rb1, ra2, rb2, fin, it_send, it_recv, it_pass, it_last, ig,
    local_sem, send_sem, recv_sem, out_sem,
):
    node = lax.axis_index("nodes")
    head = lax.axis_index("heads")
    core = lax.rem(node, 2)
    z = lax.rem(node // 2, NZ)
    y = node // (2 * NZ)
    nodes = 2 * NZ * NY
    xx = head // 2
    yl = lax.rem(head, 2)

    def at_z(d):
        return lax.rem(z + d, NZ)

    def at_y(d):
        return lax.rem(y + d, NY)

    def at_x(d):
        return lax.rem(xx + d, NX)

    left = (lax.rem(node + nodes - 1, nodes), head)
    right = (lax.rem(node + 1, nodes), head)
    other = (node + 1 - 2 * core, head)

    def z_dev(d):
        return ((y * NZ + at_z(d)) * 2 + core, head)

    def y_dev(d):
        return ((at_y(d) * NZ + z) * 2 + core, head)

    def x_dev(d):
        return (node, at_x(d) * 2 + yl)

    mate_head = xx * 2 + 1 - yl
    mate = (node, mate_head)

    partners = [z_dev(d) for d in Z_ORDER] + [y_dev(d) for d in Y_ORDER]
    partners += [x_dev(d) for d in X_ORDER] + [mate, left, right]
    barrier = pltpu.get_barrier_semaphore()
    for dev in partners:
        pl.semaphore_signal(barrier, inc=1, device_id=dev, device_id_type=MESH)

    loads = [
        pltpu.make_async_copy(x_in, xg.at[head], local_sem.at[0]),
        pltpu.make_async_copy(wk_in, wkv.at[:, 0:COLS], local_sem.at[1]),
        pltpu.make_async_copy(wv_in, wkv.at[:, COLS:], local_sem.at[2]),
        pltpu.make_async_copy(wq_in, wq, local_sem.at[3]),
        pltpu.make_async_copy(g_in, gg.at[head], local_sem.at[4]),
        pltpu.make_async_copy(wo_in, wo, local_sem.at[5]),
    ]
    for load in loads:
        load.start()
    live = live_in[0]
    lane_row = lax.broadcasted_iota(jnp.int32, (16, ROWS), 1)
    kv[1, ROWS : ROWS + 16, :] = jnp.where(lane_row < live, 1.0, 0.0).astype(BF)

    pl.semaphore_wait(barrier, len(partners))
    copies = Copies(send_sem, recv_sem)
    far = at_x(2) * 2 + yl
    x_b = {2: copies.remote(x_in, xg.at[head], x_dev(2))}
    x_a = copies.remote(x_in, xg.at[head], mate)
    for d in (1, 3):
        x_b[d] = copies.remote(x_in, xg.at[head], x_dev(d))
    g_a = copies.remote(g_in, gg.at[head], mate)
    for load in loads:
        load.wait()

    x_a.wait_recv()
    x_c = [copies.remote(xg.at[mate_head], xg.at[mate_head], x_dev(d)) for d in (1, 3)]
    x_b[2].wait_recv()
    x_d = copies.remote(xg.at[far], xg.at[far], mate)
    g_b = {d: copies.remote(g_in, gg.at[head], x_dev(d)) for d in X_ORDER}
    g_a.wait_recv()
    g_c = [copies.remote(gg.at[mate_head], gg.at[mate_head], x_dev(d)) for d in (1, 3)]
    for s in range(SHARDS):
        rows, cols = slice(s * COLS, (s + 1) * COLS), slice((s % 2) * COLS, (s % 2 + 1) * COLS)
        w_t[s // 2, 0:COLS, cols] = wq[rows, :].T
        w_t[s // 2, COLS:, cols] = wkv[rows, :].T
    for copy in (x_b[1], x_b[3], x_c[0], x_c[1], x_d):
        copy.wait_recv()

    x_full = jnp.concatenate([xg[s] for s in range(SHARDS)], axis=1)
    kv[1, 0:ROWS, :] = mm(x_full, wkv[...]).astype(BF)
    kv_right = copies.remote(kv.at[1], kv.at[0], right)
    kv_left = copies.remote(kv.at[1], kv.at[2], left)
    x_core = copies.remote(xg, xo, other)
    g_b[2].wait_recv()
    g_d = copies.remote(gg.at[far], gg.at[far], mate)

    first = lax.broadcasted_iota(jnp.int32, (ROWS, COLS), 1) < HEAD_DIM
    queries = mm(x_full, wq[...])
    qs[0:ROWS, :] = jnp.where(first, queries, 0.0).astype(BF)
    qs[ROWS:, :] = jnp.where(first, 0.0, queries).astype(BF)

    col = lax.broadcasted_iota(jnp.int32, (ROWS, ROWS), 1)
    row = lax.broadcasted_iota(jnp.int32, (ROWS, ROWS), 0)
    col_block = lax.broadcasted_iota(jnp.int32, (1, ROWS), 1) // BLOCK

    def exponents(i):
        live_row = kv[i, ROWS : ROWS + 16, :].astype(F32)[0:1, :]
        block = col_block + 2 * (node - 1 + i)
        usable = []
        for b in range(2):
            chosen = (block == win_in[b, 0]) | (block == win_in[b, 1]) | (block == win_in[b, 2])
            usable.append(jnp.broadcast_to(jnp.where(chosen, live_row, 0.0), (BLOCK, ROWS)))
        allowed = jnp.concatenate(usable, axis=0) > 0.5
        if i == 1:
            allowed = allowed | (col == row)
        sums = []
        for h in range(2):
            rows = slice(h * ROWS, (h + 1) * ROWS)
            scores = mm_nt(qs[rows, :], kv[i, 0:ROWS, 0:COLS]) * SCALE
            value = jnp.where(allowed, jnp.exp(scores), 0.0)
            expo[i, rows, :] = value
            sums.append(jnp.sum(value, axis=-1, keepdims=True))
        return jnp.concatenate(sums, axis=0)

    total = exponents(1)
    for s in range(SHARDS):
        wo_t[s * COLS : (s + 1) * COLS, :] = wo[:, s * COLS : (s + 1) * COLS].T
    for s in range(SHARDS):
        xt[s, :, 0:ROWS] = xg[s].T
    for copy in (g_b[1], g_b[3], g_c[0], g_c[1], g_d):
        copy.wait_recv()
    g_core = copies.planned(gg, go, other)

    @pl.when(core == 0)
    def _():
        g_core.start()

    g_full = jnp.concatenate([gg[s] for s in range(SHARDS)], axis=1)
    back = mm(g_full, wo_t[...])
    bs[0:ROWS, :] = jnp.where(first, back, 0.0).astype(BF)
    bs[ROWS:, :] = jnp.where(first, 0.0, back).astype(BF)
    dprob[1] = mm_nt(bs[...], kv[1, 0:ROWS, COLS:])
    x_core.wait_recv()
    for s in range(SHARDS):
        xt[s, :, ROWS:] = xo[s].T

    kv_right.wait_recv()
    kv_left.wait_recv()
    total = total + exponents(0) + exponents(2)
    inverse = 1.0 / total
    delta = 0.0
    for i in (1, 0, 2):
        vals = kv[i, 0:ROWS, COLS:]
        prob = expo[i] * inverse
        expo[i] = prob
        if i != 1:
            dprob[i] = mm_nt(bs[...], vals)
        delta = delta + jnp.sum(prob * dprob[i], axis=-1, keepdims=True)

    qs_t, bs_t = qs[...].T, bs[...].T

    def backward(i):
        prob = expo[i]
        dscore = (SCALE * prob * (dprob[i] - delta)).astype(BF)
        low = prob.astype(BF)
        term = mm(dscore, kv[i, 0:ROWS, 0:COLS])
        out = mm(low, kv[i, 0:ROWS, COLS:])
        return mm(qs_t, dscore), mm(bs_t, low), term, out

    dk, dv, dq0, at0 = backward(0)
    dkv_send[0, :, 0:COLS] = dk.astype(BF).T
    dkv_send[0, :, COLS:] = dv.astype(BF).T
    dkv_left = copies.remote(dkv_send.at[0], dkv_recv.at[0], left)
    dk, dv, dq2, at2 = backward(2)
    dkv_send[1, :, 0:COLS] = dk.astype(BF).T
    dkv_send[1, :, COLS:] = dv.astype(BF).T
    dkv_right = copies.remote(dkv_send.at[1], dkv_recv.at[1], right)
    dk, dv, dq1, at1 = backward(1)
    dq = dq0 + dq1 + dq2
    at = at0 + at1 + at2
    ad[0] = jnp.where(first, dq[0:ROWS], dq[ROWS:]).astype(BF)
    ad[1] = jnp.where(first, at[0:ROWS], at[ROWS:]).astype(BF)
    early_copy = copies.remote(ad.at[1 - core], ad_other, other)
    dkv_own[:, 0:COLS] = dk.T
    dkv_own[:, COLS:] = dv.T

    def pair(i):
        return pl.ds(2 * i, 2)

    def reduce_within(e):
        a = [
            copies.remote(part.at[e, at_z(d), 0:TOP, :], ra1.at[e, d], z_dev(d)) for d in Z_ORDER
        ]
        b = [
            copies.remote(part.at[e, pair(at_y(d)), TOP:, :], rb1.at[e, d], y_dev(d))
            for d in Y_ORDER
        ]
        return a, b

    def exchange(e, a, b):
        for copy in b:
            copy.wait_recv()
        total = part[e, pair(y), TOP:, :].astype(F32)
        for d in range(1, NY):
            total = total + rb1[e, d].astype(F32)
        rb2[e, z] = total.astype(BF)
        ref = rb2.at[e, z]
        b = [copies.remote(ref, ref, z_dev(d)) for d in Z_ORDER]
        for copy in a:
            copy.wait_recv()
        total = part[e, z, 0:TOP, :].astype(F32)
        for d in range(1, NZ):
            total = total + ra1[e, d].astype(F32)
        ra2[e, y] = total.astype(BF)
        ref = ra2.at[e, y]
        a = [copies.remote(ref, ref, y_dev(d)) for d in Y_ORDER]
        return a, b

    def gather(e, a, b):
        for copy in a:
            copy.wait_recv()
        total = ra2[e, 0].astype(F32)
        for i in range(1, NY):
            total = total + ra2[e, i].astype(F32)
        fin[e, z, 0:TOP, :] = total.astype(BF)
        ref = fin.at[e, z, 0:TOP, :]
        a = [copies.remote(ref, ref, z_dev(d)) for d in Z_ORDER]
        for copy in b:
            copy.wait_recv()
        total = rb2[e, 0].astype(F32)
        for i in range(1, NZ):
            total = total + rb2[e, i].astype(F32)
        fin[e, pair(y), TOP:, :] = total.astype(BF)
        ref = fin.at[e, pair(y), TOP:, :]
        b = [copies.remote(ref, ref, y_dev(d)) for d in Y_ORDER]
        return a, b

    def hand(e, a, b):
        mine = 2 * e + core

        def top(i):
            return copies.remote(fin.at[e, i, 0:TOP, :], f_out.at[mine, i, 0:TOP, :], other)

        def rest(i):
            return copies.remote(fin.at[e, pair(i), TOP:, :], f_out.at[mine, pair(i), TOP:, :], other)

        handed = [top(z), rest(y)]
        for d, copy in reversed(list(zip(Z_ORDER, a))):
            copy.wait_recv()
            handed.append(top(at_z(NZ - d)))
        for d, copy in reversed(list(zip(Y_ORDER, b))):
            copy.wait_recv()
            handed.append(rest(at_y(NY - d)))
        out = pltpu.make_async_copy(fin.at[e], f_out.at[mine], out_sem.at[e])
        out.start()
        return handed, out

    early_copy.wait_recv()

    @pl.when(core == 0)
    def _():
        part[0, :, :, :] = (
            mm(
                xt[...].reshape(SHARDS * COLS, 2 * ROWS),
                jnp.concatenate([ad[0], ad_other[...]], axis=0),
            )
            .astype(BF)
            .reshape(SHARDS, COLS, COLS)
        )

    @pl.when(core == 1)
    def _():
        g_core.wait_recv()
        lhs = jnp.concatenate([ad[1].T, ad_other[...].T], axis=1)
        for s in range(SHARDS):
            part[0, s] = mm(lhs, jnp.concatenate([gg[s], go[s]], axis=0)).astype(BF)

    early = reduce_within(0)
    dkv_left.wait_recv()
    dkv_right.wait_recv()
    dkv = dkv_own[...] + dkv_recv[0].astype(F32) + dkv_recv[1].astype(F32)
    grads[0] = dkv[:, 0:COLS].astype(BF)
    grads[1] = dkv[:, COLS:].astype(BF)
    late_copy = copies.remote(grads.at[1 - core], late_other, other)

    all_grads = jnp.concatenate([ad[0], grads[0], grads[1]], axis=1)
    it_copies = []
    for d in X_ORDER:
        terms = mm(all_grads, w_t[at_x(d)]).astype(BF)
        it_send[d, 0] = terms[:, 0:COLS]
        it_send[d, 1] = terms[:, COLS:]
        it_copies.append(copies.remote(it_send.at[d], it_recv.at[d], x_dev(d)))

    late_copy.wait_recv()
    part[1, :, :, :] = (
        mm(
            xt[...].reshape(SHARDS * COLS, 2 * ROWS),
            jnp.concatenate([grads[core], late_other[...]], axis=0),
        )
        .astype(BF)
        .reshape(SHARDS, COLS, COLS)
    )
    late = reduce_within(1)
    early = exchange(0, *early)
    late = exchange(1, *late)
    early = gather(0, *early)

    it_own = mm(all_grads, w_t[xx])
    low, high = it_own[:, 0:COLS], it_own[:, COLS:]
    for copy in it_copies:
        copy.wait_recv()
    for d in range(1, NX):
        low = low + it_recv[d, 0].astype(F32)
        high = high + it_recv[d, 1].astype(F32)
    is_low = jnp.full((ROWS, COLS), yl, jnp.int32) == 0
    it_pass[...] = jnp.where(is_low, high, low).astype(BF)
    it_copy = copies.remote(it_pass, it_last, mate)

    late = gather(1, *late)
    it_copy.wait_recv()
    ig[...] = (jnp.where(is_low, low, high) + it_last[...].astype(F32)).astype(BF)
    ig_copy = pltpu.make_async_copy(ig, ig_out, out_sem.at[2])
    ig_copy.start()

    early_handed, early_out = hand(0, *early)
    late_handed, late_out = hand(1, *late)
    for copy in early_handed + late_handed:
        copy.wait_recv()
    for copy in copies.started:
        copy.wait_send()

    @pl.when(core == 0)
    def _():
        g_core.wait_send()

    for out in (ig_copy, early_out, late_out):
        out.wait()


N_COPIES = 14 + 4 + 4 + 4 + 2 * 3 * (NZ - 1 + NY - 1) + 2 * (NZ + NY)


def hand_out(ig_in, f_in, ig_out, q_out, k_out, v_out, o_out, ig, fin, sem):
    loads = [pltpu.make_async_copy(f_in.at[i], fin.at[i], sem.at[i]) for i in range(4)]
    loads.append(pltpu.make_async_copy(ig_in, ig, sem.at[4]))
    for load in loads:
        load.start()
    stores = [[(fin.at[0], q_out)]]
    stores.append([(fin.at[1, s], o_out.at[:, s * COLS : (s + 1) * COLS]) for s in range(SHARDS)])
    stores += [[(fin.at[2], k_out)], [(fin.at[3], v_out)], [(ig, ig_out)]]
    started = []
    for load, pairs in zip(loads, stores):
        load.wait()
        for src, dst in pairs:
            started.append(pltpu.make_async_copy(src, dst, sem.at[5 + len(started)]))
            started[-1].start()
    for store in started:
        store.wait()


def body(inputs, out_grad, w_query, w_key, w_value, w_out, live_rows, window_blocks):
    anyspec = pl.BlockSpec(memory_space=pl.ANY)
    smem = pl.BlockSpec(memory_space=pltpu.SMEM)
    vm = pltpu.VMEM
    params = pltpu.CompilerParams(
        collective_id=0, has_side_effects=True, vmem_limit_bytes=62 * 1024 * 1024
    )
    input_grad, fin = pl.pallas_call(
        kernel,
        out_shape=(
            jax.ShapeDtypeStruct((ROWS, COLS), BF),
            jax.ShapeDtypeStruct((4, SHARDS, BLOCK, COLS), BF),
        ),
        in_specs=[anyspec] * 6 + [smem] * 2,
        out_specs=(anyspec, anyspec),
        scratch_shapes=[
            vm((SHARDS, ROWS, COLS), BF),
            vm((SHARDS, ROWS, COLS), BF),
            vm((SHARDS, ROWS, COLS), BF),
            vm((SHARDS, ROWS, COLS), BF),
            vm((SHARDS, COLS, 2 * ROWS), BF),
            vm((SHARDS * COLS, COLS), BF),
            vm((SHARDS * COLS, 2 * COLS), BF),
            vm((NX, 3 * COLS, 2 * COLS), BF),
            vm((COLS, SHARDS * COLS), BF),
            vm((SHARDS * COLS, COLS), BF),
            vm((3, ROWS + 16, 2 * COLS), BF),
            vm((2 * ROWS, COLS), BF),
            vm((2 * ROWS, COLS), BF),
            vm((3, 2 * ROWS, ROWS), F32),
            vm((3, 2 * ROWS, ROWS), F32),
            vm((2, ROWS, COLS), BF),
            vm((ROWS, COLS), BF),
            vm((ROWS, COLS), BF),
            vm((ROWS, 2 * COLS), F32),
            vm((2, ROWS, 2 * COLS), BF),
            vm((2, ROWS, 2 * COLS), BF),
            vm((2, ROWS, COLS), BF),
            vm((2, SHARDS, BLOCK, COLS), BF),
            vm((2, NZ, TOP, COLS), BF),
            vm((2, NY, 2, BLOCK - TOP, COLS), BF),
            vm((2, NY, TOP, COLS), BF),
            vm((2, NZ, 2, BLOCK - TOP, COLS), BF),
            vm((2, SHARDS, BLOCK, COLS), BF),
            vm((NX, 2, ROWS, COLS), BF),
            vm((NX, 2, ROWS, COLS), BF),
            vm((ROWS, COLS), BF),
            vm((ROWS, COLS), BF),
            vm((ROWS, COLS), BF),
            pltpu.SemaphoreType.DMA((6,)),
            pltpu.SemaphoreType.DMA((N_COPIES,)),
            pltpu.SemaphoreType.DMA((N_COPIES,)),
            pltpu.SemaphoreType.DMA((3,)),
        ],
        compiler_params=params,
        cost_estimate=pl.CostEstimate(
            flops=1200000000, bytes_accessed=3000000, transcendentals=400000
        ),
    )(inputs, out_grad, w_query, w_key, w_value, w_out, live_rows, window_blocks)
    width = SHARDS * COLS
    cols = jax.ShapeDtypeStruct((SHARDS, COLS, COLS), BF)
    input_grad, grad_query, grad_key, grad_value, grad_out = pl.pallas_call(
        hand_out,
        out_shape=(
            jax.ShapeDtypeStruct((ROWS, COLS), BF),
            cols,
            cols,
            cols,
            jax.ShapeDtypeStruct((COLS, width), BF),
        ),
        in_specs=[anyspec] * 2,
        out_specs=[anyspec] * 5,
        scratch_shapes=[
            vm((ROWS, COLS), BF),
            vm((4, SHARDS, BLOCK, COLS), BF),
            pltpu.SemaphoreType.DMA((9 + SHARDS,)),
        ],
        compiler_params=pltpu.CompilerParams(vmem_limit_bytes=62 * 1024 * 1024),
        cost_estimate=pl.CostEstimate(flops=0, bytes_accessed=2200000, transcendentals=0),
    )(input_grad, fin)
    return (
        input_grad,
        grad_query.reshape(width, COLS),
        grad_key.reshape(width, COLS),
        grad_value.reshape(width, COLS),
        grad_out,
    )


def solution(mesh):
    placed = (
        P("nodes", "heads"),
        P("nodes", "heads"),
        P(None, "heads"),
        P(None, "heads"),
        P(None, "heads"),
        P("heads", None),
        P("nodes"),
        P("nodes", None),
    )
    return jax.shard_map(
        body,
        mesh=mesh,
        in_specs=placed,
        out_specs=(
            P("nodes", "heads"),
            P(None, "heads"),
            P(None, "heads"),
            P(None, "heads"),
            P("heads", None),
        ),
        check_vma=False,
    )
```

time: 107 us -> 67.9 us (0.63)
  the two profiles are of different devices: /device:TPU:9 before, /device:TPU:1 now
where the time goes in v3:
time: 67.9 us; the launch traced here: 67.6 us
  Pallas kernels  66.3 us (98%)
  between operations  1.29 us (2%)
    pallas_call x1, Pallas kernels, body(): pl.pallas_call(kernel, out_shape=(jax.ShapeDtypeStruct((ROWS, COLS), BF),...  64.2 us
    pallas_call x1, Pallas kernels, body(): pl.pallas_call(hand_out, out_shape=(jax.ShapeDtypeStruct((ROWS, COLS), BF...  2.07 us

profile of v3, /device:TPU:1, one launch (start us, length us, event | category | flops | bytes accessed | tf_op | source)
XLA Modules:
  0.0 67.6 jit_solution(7395323084824991235)
XLA Ops:
  1.3 64.2 %shard_map.119 = (bf16[256,128]{1,0:T(8,128)(2,1)}, bf16[4,8,128,128]{3,2,1,0:T(8,128)(2,1)}) custom-call(bf16[256,128]{1,0:T(8,128)(2,1)} %x_in.1, bf16[256,128]{1,0:T(8,128)(2,1)} %g_in.1, bf16[1024,128]{1,0:T(8,128)(2,1)} %wq_in.1, bf16[1024,128]{1,0:T(8,128)(2,1)} %wk_in.1, bf16[1024,128]{1,0:T(8,128)(2,1)} %wv_in.1, bf16[128,1024]{1,0:T(8,128)(2,1)} %wo_in.1, ...), custom_call_target="tpu_custom_call" | custom-call | flops 1200000000 | bytes 3000000 | tf_op jit(solution)/shard_map/pallas_call | solution.py:431
  65.5 2.1 %shard_map.120 = (bf16[256,128]{1,0:T(8,128)(2,1)}, bf16[8,128,128]{2,1,0:T(8,128)(2,1)}, bf16[8,128,128]{2,1,0:T(8,128)(2,1)}, bf16[8,128,128]{2,1,0:T(8,128)(2,1)}, bf16[128,1024]{1,0:T(8,128)(2,1)}) custom-call(bf16[256,128]{1,0:T(8,128)(2,1)} %get-tuple-element.12.ig_in, bf16[4,8,128,128]{3,2,1,0:T(8,128)(2,1)} %get-tuple-element.13.f_in), custom_call_target="tpu_custom_call" | custom-call | bytes 2200000 | tf_op jit(solution)/shard_map/pallas_call | solution.py:485

commit v4 on v3

v4 whole, which is shorter than its diff:
```python
import math

import jax
import jax.numpy as jnp
from jax import lax
from jax.experimental import pallas as pl
from jax.experimental.pallas import tpu as pltpu
from jax.sharding import PartitionSpec as P

HEAD_DIM = 64
BLOCK = 128
ROWS = 256
COLS = 128
SHARDS = 8
NZ = 8
NY = 4
NX = 4
Z_ORDER = (4, 3, 5, 2, 6, 1, 7)
Y_ORDER = (2, 1, 3)
X_ORDER = (2, 1, 3)
TOPS = (64, 80)
PIECE = 16
SCALE = HEAD_DIM ** (-0.5)
BF = jnp.bfloat16
F32 = jnp.float32
MESH = pl.DeviceIdType.MESH
NT = (((1,), (1,)), ((), ()))
TN = (((0,), (0,)), ((), ()))


def mm(a, b):
    return jnp.dot(a, b, preferred_element_type=F32)


def mm_nt(a, b):
    return lax.dot_general(a, b, NT, preferred_element_type=F32)


def mm_tn(a, b):
    return lax.dot_general(a, b, TN, preferred_element_type=F32)


def rows_of(ref):
    return math.prod(ref.shape) // COLS


class Group:
    def __init__(self, copies, index):
        self.copies, self.index, self.rows = copies, index, 0

    def send(self, src, dst, device):
        self.rows += rows_of(src)
        pltpu.make_async_remote_copy(
            src_ref=src,
            dst_ref=dst,
            send_sem=self.copies.pool(rows_of(src)),
            recv_sem=self.copies.recv.at[self.index],
            device_id=device,
            device_id_type=MESH,
        ).start()
        return self

    def wait(self):
        ref = self.copies.tally.at[0 : self.rows, :]
        pltpu.make_async_copy(ref, ref, self.copies.recv.at[self.index]).wait()


class Copies:
    def __init__(self, send, recv, tally):
        self.send, self.recv, self.tally = send, recv, tally
        self.groups, self.pools = 0, [0]

    def group(self):
        self.groups += 1
        return Group(self, self.groups - 1)

    def pool(self, rows):
        if self.pools[-1] + rows > POOL_ROWS:
            self.pools.append(0)
        self.pools[-1] += rows
        return self.send.at[len(self.pools) - 1]

    def finish(self):
        for i, rows in enumerate(self.pools):
            ref = self.tally.at[0:rows, :]
            pltpu.make_async_copy(ref, ref, self.send.at[i]).wait()


def kernel(
    x_in, g_in, wq_in, wk_in, wv_in, wo_in, live_in, win_in,
    ig_out, f_out,
    xg, gg, xo, go, xt, wq, wkv, w_t, wo, wo_t, kv, qs, bs, expo, ad, ad_other, late_other,
    dkv_own, dkv_send, dkv_recv, grads,
    part, ra1, rb1, ra2, rb2, fin, it_send, it_recv, it_pass, it_last, ig,
    ea1, eb1, ea2, es2, eb2, tally, live_s, win_s,
    local_sem, send_sem, recv_sem, pair_sem, out_sem,
):
    node = lax.axis_index("nodes")
    head = lax.axis_index("heads")
    core = lax.rem(node, 2)
    z = lax.rem(node // 2, NZ)
    y = node // (2 * NZ)
    nodes = 2 * NZ * NY
    xx = head // 2
    yl = lax.rem(head, 2)

    def at_z(d):
        return lax.rem(z + d, NZ)

    def at_y(d):
        return lax.rem(y + d, NY)

    def at_x(d):
        return lax.rem(xx + d, NX)

    left = (lax.rem(node + nodes - 1, nodes), head)
    right = (lax.rem(node + 1, nodes), head)
    other = (node + 1 - 2 * core, head)

    def z_dev(d):
        return ((y * NZ + at_z(d)) * 2 + core, head)

    def y_dev(d):
        return ((at_y(d) * NZ + z) * 2 + core, head)

    def x_dev(d):
        return (node, at_x(d) * 2 + yl)

    mate_head = xx * 2 + 1 - yl
    mate = (node, mate_head)

    partners = [z_dev(d) for d in Z_ORDER] + [y_dev(d) for d in Y_ORDER]
    partners += [x_dev(d) for d in X_ORDER] + [mate, left, right]
    barrier = pltpu.get_barrier_semaphore()
    for dev in partners:
        pl.semaphore_signal(barrier, inc=1, device_id=dev, device_id_type=MESH)

    scalars = [
        pltpu.make_async_copy(live_in, live_s, local_sem.at[0]),
        pltpu.make_async_copy(win_in, win_s, local_sem.at[1]),
    ]
    loads = [
        pltpu.make_async_copy(x_in, xg.at[head], local_sem.at[2]),
        pltpu.make_async_copy(g_in, gg.at[head], local_sem.at[2]),
        pltpu.make_async_copy(wk_in, wkv.at[:, 0:COLS], local_sem.at[3]),
        pltpu.make_async_copy(wv_in, wkv.at[:, COLS:], local_sem.at[3]),
        pltpu.make_async_copy(wq_in, wq, local_sem.at[4]),
        pltpu.make_async_copy(wo_in, wo, local_sem.at[4]),
    ]
    for load in scalars + loads:
        load.start()

    pl.semaphore_wait(barrier, len(partners))
    copies = Copies(send_sem, recv_sem, tally)
    far = at_x(2) * 2 + yl
    x_far, x_mate, x_rest = copies.group(), copies.group(), copies.group()
    x_far.send(x_in, xg.at[head], x_dev(2))
    x_mate.send(x_in, xg.at[head], mate)
    for d in (1, 3):
        x_rest.send(x_in, xg.at[head], x_dev(d))
    g_far, g_mate, g_rest = copies.group(), copies.group(), copies.group()
    g_mate.send(g_in, gg.at[head], mate)
    for load in scalars:
        load.wait()
    live = live_s[0]
    lane_row = lax.broadcasted_iota(jnp.int32, (16, ROWS), 1)
    kv[1, ROWS : ROWS + 16, :] = jnp.where(lane_row < live, 1.0, 0.0).astype(BF)
    pltpu.make_async_copy(xg.at[0:2], xg.at[0:2], local_sem.at[2]).wait()
    pltpu.make_async_copy(wkv, wkv, local_sem.at[3]).wait()
    pltpu.make_async_copy(wkv, wkv, local_sem.at[4]).wait()

    x_mate.wait()
    for d in (1, 3):
        x_rest.send(xg.at[mate_head], xg.at[mate_head], x_dev(d))
    x_far.wait()
    x_rest.send(xg.at[far], xg.at[far], mate)
    g_far.send(g_in, gg.at[head], x_dev(2))
    for d in (1, 3):
        g_rest.send(g_in, gg.at[head], x_dev(d))
    g_mate.wait()
    for d in (1, 3):
        g_rest.send(gg.at[mate_head], gg.at[mate_head], x_dev(d))
    for s in range(SHARDS):
        rows, cols = slice(s * COLS, (s + 1) * COLS), slice((s % 2) * COLS, (s % 2 + 1) * COLS)
        w_t[s // 2, 0:COLS, cols] = wq[rows, :].T
        w_t[s // 2, COLS:, cols] = wkv[rows, :].T
    x_rest.wait()

    x_full = jnp.concatenate([xg[s] for s in range(SHARDS)], axis=1)
    kv[1, 0:ROWS, :] = mm(x_full, wkv[...]).astype(BF)
    kv_halo = copies.group()
    kv_halo.send(kv.at[1], kv.at[0], right)
    kv_halo.send(kv.at[1], kv.at[2], left)
    x_core = copies.group().send(xg, xo, other)
    g_far.wait()
    g_rest.send(gg.at[far], gg.at[far], mate)

    first = lax.broadcasted_iota(jnp.int32, (ROWS, COLS), 1) < HEAD_DIM
    queries = mm(x_full, wq[...])
    qs[0:ROWS, :] = jnp.where(first, queries, 0.0).astype(BF)
    qs[ROWS:, :] = jnp.where(first, 0.0, queries).astype(BF)

    col = lax.broadcasted_iota(jnp.int32, (ROWS, ROWS), 1)
    row = lax.broadcasted_iota(jnp.int32, (ROWS, ROWS), 0)
    col_block = lax.broadcasted_iota(jnp.int32, (1, ROWS), 1) // BLOCK

    def exponents(i):
        live_row = kv[i, ROWS : ROWS + 16, :].astype(F32)[0:1, :]
        block = col_block + 2 * (node - 1 + i)
        usable = []
        for b in range(2):
            chosen = (block == win_s[b, 0]) | (block == win_s[b, 1]) | (block == win_s[b, 2])
            usable.append(jnp.broadcast_to(jnp.where(chosen, live_row, 0.0), (BLOCK, ROWS)))
        allowed = jnp.concatenate(usable, axis=0) > 0.5
        if i == 1:
            allowed = allowed | (col == row)
        sums = []
        for h in range(2):
            rows = slice(h * ROWS, (h + 1) * ROWS)
            scores = mm_nt(qs[rows, :], kv[i, 0:ROWS, 0:COLS]) * SCALE
            value = jnp.where(allowed, jnp.exp(scores), 0.0)
            expo[i, rows, :] = value
            sums.append(jnp.sum(value, axis=-1, keepdims=True))
        return jnp.concatenate(sums, axis=0)

    total = exponents(1)
    qs_t = qs[...].T
    for s in range(SHARDS):
        wo_t[s * COLS : (s + 1) * COLS, :] = wo[:, s * COLS : (s + 1) * COLS].T
    for s in range(SHARDS):
        xt[s, :, 0:ROWS] = xg[s].T
    g_rest.wait()
    g_core = pltpu.make_async_remote_copy(
        src_ref=gg,
        dst_ref=go,
        send_sem=pair_sem.at[0],
        recv_sem=pair_sem.at[1],
        device_id=other,
        device_id_type=MESH,
    )

    @pl.when(core == 0)
    def _():
        g_core.start()

    g_full = jnp.concatenate([gg[s] for s in range(SHARDS)], axis=1)
    back = mm(g_full, wo_t[...])
    bs[0:ROWS, :] = jnp.where(first, back, 0.0).astype(BF)
    bs[ROWS:, :] = jnp.where(first, 0.0, back).astype(BF)
    bs_t = bs[...].T
    x_core.wait()
    for s in range(SHARDS):
        xt[s, :, ROWS:] = xo[s].T

    def keys(i):
        return kv[i, 0:ROWS, 0:COLS]

    def vals(i):
        return kv[i, 0:ROWS, COLS:]

    dprob = {1: mm_nt(bs[...], vals(1))}
    kv_halo.wait()
    total = total + exponents(0) + exponents(2)
    inverse = 1.0 / total
    prob, low = {}, {}
    dkv_halo = copies.group()
    for j, i, dev in ((0, 0, left), (1, 2, right)):
        prob[i] = expo[i] * inverse
        low[i] = prob[i].astype(BF)
        dkv_send[j, 1] = mm(bs_t, low[i]).astype(BF).T
        dkv_halo.send(dkv_send.at[j, 1], dkv_recv.at[j, 1], dev)
    prob[1] = expo[1] * inverse
    dprob[0] = mm_nt(bs[...], vals(0))
    dprob[2] = mm_nt(bs[...], vals(2))
    delta = 0.0
    for i in range(3):
        delta = delta + jnp.sum(prob[i] * dprob[i], axis=-1, keepdims=True)
    dscore = {}
    for j, i, dev in ((0, 0, left), (1, 2, right)):
        dscore[i] = (SCALE * prob[i] * (dprob[i] - delta)).astype(BF)
        dkv_send[j, 0] = mm(qs_t, dscore[i]).astype(BF).T
        dkv_halo.send(dkv_send.at[j, 0], dkv_recv.at[j, 0], dev)

    early_copy = pltpu.make_async_remote_copy(
        src_ref=ad.at[1 - core],
        dst_ref=ad_other,
        send_sem=pair_sem.at[2],
        recv_sem=pair_sem.at[3],
        device_id=other,
        device_id_type=MESH,
    )
    low[1] = prob[1].astype(BF)
    at = mm(low[0], vals(0)) + mm(low[1], vals(1)) + mm(low[2], vals(2))
    ad[1] = jnp.where(first, at[0:ROWS], at[ROWS:]).astype(BF)

    @pl.when(core == 0)
    def _():
        early_copy.start()

    dscore[1] = (SCALE * prob[1] * (dprob[1] - delta)).astype(BF)
    dq = mm(dscore[0], keys(0)) + mm(dscore[1], keys(1)) + mm(dscore[2], keys(2))
    ad[0] = jnp.where(first, dq[0:ROWS], dq[ROWS:]).astype(BF)

    @pl.when(core == 1)
    def _():
        early_copy.start()

    dkv_own[0] = mm(qs_t, dscore[1]).T
    dkv_own[1] = mm(bs_t, low[1]).T

    def pair(i):
        return pl.ds(2 * i, 2)

    def to_all(devices, order, src, dst):
        group = copies.group()
        for d in order:
            group.send(src(d), dst(d), devices(d))
        return group

    def reduce_within(e, top, a_in, b_in):
        a = to_all(z_dev, Z_ORDER, lambda d: part.at[e, at_z(d), 0:top, :], lambda d: a_in.at[d])
        b = to_all(
            y_dev, Y_ORDER, lambda d: part.at[e, pair(at_y(d)), top:, :], lambda d: b_in.at[d]
        )
        return a, b

    def added(own, arrived, count):
        total = own.astype(F32)
        for d in range(1, count):
            total = total + arrived[d].astype(F32)
        return total.astype(BF)

    def added_in_order(copies_in, count):
        total = copies_in[0].astype(F32)
        for i in range(1, count):
            total = total + copies_in[i].astype(F32)
        return total.astype(BF)

    def spread(devices, order, ref):
        return to_all(devices, order, lambda d: ref, lambda d: ref)

    def hand(e, a, b):
        mine, top = 2 * e + core, TOPS[e]
        group = copies.group()
        b.wait()
        group.send(fin.at[e, :, top:, :], f_out.at[mine, :, top:, :], other)
        a.wait()
        group.send(fin.at[e, :, 0:top, :], f_out.at[mine, :, 0:top, :], other)
        out = pltpu.make_async_copy(fin.at[e], f_out.at[mine], out_sem.at[e])
        out.start()
        return group, out

    early_copy.wait_recv()

    @pl.when(core == 0)
    def _():
        part[0, :, :, :] = (
            mm(
                xt[...].reshape(SHARDS * COLS, 2 * ROWS),
                jnp.concatenate([ad[0], ad_other[...]], axis=0),
            )
            .astype(BF)
            .reshape(SHARDS, COLS, COLS)
        )

    @pl.when(core == 1)
    def _():
        g_core.wait_recv()
        lhs = jnp.concatenate([ad[1].T, ad_other[...].T], axis=1)
        for s in range(SHARDS):
            part[0, s] = mm(lhs, jnp.concatenate([gg[s], go[s]], axis=0)).astype(BF)

    early_a, early_b = reduce_within(0, TOPS[0], ea1, eb1)
    dkv_halo.wait()
    for i in range(2):
        grads[i] = (dkv_own[i] + dkv_recv[0, i].astype(F32) + dkv_recv[1, i].astype(F32)).astype(BF)
    late_copy = copies.group().send(grads.at[1 - core], late_other, other)

    all_grads = jnp.concatenate([ad[0], grads[0], grads[1]], axis=1)
    it_copies = copies.group()
    for d in X_ORDER:
        terms = mm(all_grads, w_t[at_x(d)]).astype(BF)
        it_send[d, 0] = terms[:, 0:COLS]
        it_send[d, 1] = terms[:, COLS:]
        it_copies.send(it_send.at[d], it_recv.at[d], x_dev(d))

    late_copy.wait()
    part[1, :, :, :] = (
        mm(
            xt[...].reshape(SHARDS * COLS, 2 * ROWS),
            jnp.concatenate([grads[core], late_other[...]], axis=0),
        )
        .astype(BF)
        .reshape(SHARDS, COLS, COLS)
    )
    late_a, late_b = reduce_within(1, TOPS[1], ra1, rb1)

    top = TOPS[0]
    early_a.wait()
    ea2[y] = added(part[0, z, 0:top, :], ea1, NZ)
    early_a = spread(y_dev, Y_ORDER, ea2.at[y])
    early_b.wait()
    es2[...] = added(part[0, pair(y), top:, :], eb1, NY)

    def piece(i):
        return lax.rem(i, 4) * PIECE

    def es2_piece(d):
        i = at_z(d)
        return es2.at[i // 4, pl.ds(pl.multiple_of(piece(i), PIECE), PIECE), :]

    early_b = to_all(z_dev, Z_ORDER, es2_piece, lambda d: eb2.at[d])

    late_b.wait()
    rb2[z] = added(part[1, pair(y), TOPS[1] :, :], rb1, NY)
    late_b = spread(z_dev, Z_ORDER, rb2.at[z])
    late_a.wait()
    ra2[y] = added(part[1, z, 0 : TOPS[1], :], ra1, NZ)
    late_a = spread(y_dev, Y_ORDER, ra2.at[y])

    early_b.wait()
    own_piece = pl.ds(pl.multiple_of(piece(z), PIECE), PIECE)
    place = pl.ds(pl.multiple_of(top + piece(z), PIECE), PIECE)
    fin[0, 2 * y + z // 4, place, :] = added(es2[z // 4, own_piece, :], eb2, NZ)
    early_b = spread(z_dev, Z_ORDER, fin.at[0, 2 * y + z // 4, place, :])
    early_a.wait()
    fin[0, z, 0:top, :] = added_in_order(ea2, NY)
    early_a = spread(z_dev, Z_ORDER, fin.at[0, z, 0:top, :])

    it_own = mm(all_grads, w_t[xx])
    low_half, high_half = it_own[:, 0:COLS], it_own[:, COLS:]
    it_copies.wait()
    for d in range(1, NX):
        low_half = low_half + it_recv[d, 0].astype(F32)
        high_half = high_half + it_recv[d, 1].astype(F32)
    is_low = jnp.full((ROWS, COLS), yl, jnp.int32) == 0
    it_pass[...] = jnp.where(is_low, high_half, low_half).astype(BF)
    it_copy = copies.group().send(it_pass, it_last, mate)

    late_a.wait()
    fin[1, z, 0 : TOPS[1], :] = added_in_order(ra2, NY)
    late_a = spread(z_dev, Z_ORDER, fin.at[1, z, 0 : TOPS[1], :])
    early_b.wait()
    early_b = spread(y_dev, Y_ORDER, fin.at[0, pair(y), top:, :])
    late_b.wait()
    fin[1, pair(y), TOPS[1] :, :] = added_in_order(rb2, NZ)
    late_b = spread(y_dev, Y_ORDER, fin.at[1, pair(y), TOPS[1] :, :])
    it_copy.wait()
    ig[...] = (jnp.where(is_low, low_half, high_half) + it_last[...].astype(F32)).astype(BF)
    ig_copy = pltpu.make_async_copy(ig, ig_out, out_sem.at[2])
    ig_copy.start()

    early_handed, early_out = hand(0, early_a, early_b)
    late_handed, late_out = hand(1, late_a, late_b)
    early_handed.wait()
    late_handed.wait()
    copies.finish()
    early_copy.wait_send()

    @pl.when(core == 0)
    def _():
        g_core.wait_send()

    for out in (ig_copy, early_out, late_out):
        out.wait()


POOL_ROWS = 2560
N_GROUPS = 27
N_POOLS = 7


def hand_out(ig_in, f_in, ig_out, q_out, k_out, v_out, o_out, ig, fin, sem):
    loads = [pltpu.make_async_copy(f_in.at[i], fin.at[i], sem.at[i]) for i in range(4)]
    loads.append(pltpu.make_async_copy(ig_in, ig, sem.at[4]))
    for load in loads:
        load.start()
    stores = [[(fin.at[0], q_out)]]
    stores.append([(fin.at[1, s], o_out.at[:, s * COLS : (s + 1) * COLS]) for s in range(SHARDS)])
    stores += [[(fin.at[2], k_out)], [(fin.at[3], v_out)], [(ig, ig_out)]]
    started = []
    for load, pairs in zip(loads, stores):
        load.wait()
        for src, dst in pairs:
            started.append(pltpu.make_async_copy(src, dst, sem.at[5 + len(started)]))
            started[-1].start()
    for store in started:
        store.wait()


def body(inputs, out_grad, w_query, w_key, w_value, w_out, live_rows, window_blocks):
    anyspec = pl.BlockSpec(memory_space=pl.ANY)
    vm = pltpu.VMEM
    params = pltpu.CompilerParams(
        collective_id=0, has_side_effects=True, vmem_limit_bytes=62 * 1024 * 1024
    )
    input_grad, fin = pl.pallas_call(
        kernel,
        out_shape=(
            jax.ShapeDtypeStruct((ROWS, COLS), BF),
            jax.ShapeDtypeStruct((4, SHARDS, BLOCK, COLS), BF),
        ),
        in_specs=[anyspec] * 8,
        out_specs=(anyspec, anyspec),
        scratch_shapes=[
            vm((SHARDS, ROWS, COLS), BF),
            vm((SHARDS, ROWS, COLS), BF),
            vm((SHARDS, ROWS, COLS), BF),
            vm((SHARDS, ROWS, COLS), BF),
            vm((SHARDS, COLS, 2 * ROWS), BF),
            vm((SHARDS * COLS, COLS), BF),
            vm((SHARDS * COLS, 2 * COLS), BF),
            vm((NX, 3 * COLS, 2 * COLS), BF),
            vm((COLS, SHARDS * COLS), BF),
            vm((SHARDS * COLS, COLS), BF),
            vm((3, ROWS + 16, 2 * COLS), BF),
            vm((2 * ROWS, COLS), BF),
            vm((2 * ROWS, COLS), BF),
            vm((3, 2 * ROWS, ROWS), F32),
            vm((2, ROWS, COLS), BF),
            vm((ROWS, COLS), BF),
            vm((ROWS, COLS), BF),
            vm((2, ROWS, COLS), F32),
            vm((2, 2, ROWS, COLS), BF),
            vm((2, 2, ROWS, COLS), BF),
            vm((2, ROWS, COLS), BF),
            vm((2, SHARDS, BLOCK, COLS), BF),
            vm((NZ, TOPS[1], COLS), BF),
            vm((NY, 2, BLOCK - TOPS[1], COLS), BF),
            vm((NY, TOPS[1], COLS), BF),
            vm((NZ, 2, BLOCK - TOPS[1], COLS), BF),
            vm((2, SHARDS, BLOCK, COLS), BF),
            vm((NX, 2, ROWS, COLS), BF),
            vm((NX, 2, ROWS, COLS), BF),
            vm((ROWS, COLS), BF),
            vm((ROWS, COLS), BF),
            vm((ROWS, COLS), BF),
            vm((NZ, TOPS[0], COLS), BF),
            vm((NY, 2, BLOCK - TOPS[0], COLS), BF),
            vm((NY, TOPS[0], COLS), BF),
            vm((2, BLOCK - TOPS[0], COLS), BF),
            vm((NZ, PIECE, COLS), BF),
            vm((POOL_ROWS, COLS), BF),
            pltpu.SMEM((1,), jnp.int32),
            pltpu.SMEM((2, 3), jnp.int32),
            pltpu.SemaphoreType.DMA((5,)),
            pltpu.SemaphoreType.DMA((N_POOLS,)),
            pltpu.SemaphoreType.DMA((N_GROUPS,)),
            pltpu.SemaphoreType.DMA((4,)),
            pltpu.SemaphoreType.DMA((3,)),
        ],
        compiler_params=params,
        cost_estimate=pl.CostEstimate(
            flops=1200000000, bytes_accessed=3000000, transcendentals=400000
        ),
    )(inputs, out_grad, w_query, w_key, w_value, w_out, live_rows, window_blocks)
    width = SHARDS * COLS
    cols = jax.ShapeDtypeStruct((SHARDS, COLS, COLS), BF)
    input_grad, grad_query, grad_key, grad_value, grad_out = pl.pallas_call(
        hand_out,
        out_shape=(
            jax.ShapeDtypeStruct((ROWS, COLS), BF),
            cols,
            cols,
            cols,
            jax.ShapeDtypeStruct((COLS, width), BF),
        ),
        in_specs=[anyspec] * 2,
        out_specs=[anyspec] * 5,
        scratch_shapes=[
            vm((ROWS, COLS), BF),
            vm((4, SHARDS, BLOCK, COLS), BF),
            pltpu.SemaphoreType.DMA((9 + SHARDS,)),
        ],
        compiler_params=pltpu.CompilerParams(vmem_limit_bytes=62 * 1024 * 1024),
        cost_estimate=pl.CostEstimate(flops=0, bytes_accessed=2200000, transcendentals=0),
    )(input_grad, fin)
    return (
        input_grad,
        grad_query.reshape(width, COLS),
        grad_key.reshape(width, COLS),
        grad_value.reshape(width, COLS),
        grad_out,
    )


def solution(mesh):
    placed = (
        P("nodes", "heads"),
        P("nodes", "heads"),
        P(None, "heads"),
        P(None, "heads"),
        P(None, "heads"),
        P("heads", None),
        P("nodes"),
        P("nodes", None),
    )
    return jax.shard_map(
        body,
        mesh=mesh,
        in_specs=placed,
        out_specs=(
            P("nodes", "heads"),
            P(None, "heads"),
            P(None, "heads"),
            P(None, "heads"),
            P("heads", None),
        ),
        check_vma=False,
    )
```

time: 67.9 us -> 65.9 us (0.971)
  Pallas kernels: 66.3 us -> 64.5 us
    pallas_call x1, Pallas kernels: 64.2 us -> 62.4 us  [body(): pl.pallas_call(kernel, out_shape=(jax.ShapeDtypeStruct((ROWS, COLS), BF),...]
where the time goes in v4:
time: 65.9 us; the launch traced here: 65.8 us
  Pallas kernels  64.5 us (98%)
  between operations  1.29 us (2%)
    pallas_call x1, Pallas kernels, body(): pl.pallas_call(kernel, out_shape=(jax.ShapeDtypeStruct((ROWS, COLS), BF),...  62.4 us
    pallas_call x1, Pallas kernels, body(): pl.pallas_call(hand_out, out_shape=(jax.ShapeDtypeStruct((ROWS, COLS), BF...  2.07 us

profile of v4, /device:TPU:1, one launch (start us, length us, event | category | flops | bytes accessed | tf_op | source)
XLA Modules:
  0.0 65.8 jit_solution(984967656309603870)
XLA Ops:
  1.3 62.4 %shard_map.119 = (bf16[256,128]{1,0:T(8,128)(2,1)}, bf16[4,8,128,128]{3,2,1,0:T(8,128)(2,1)}) custom-call(bf16[256,128]{1,0:T(8,128)(2,1)} %x_in.1, bf16[256,128]{1,0:T(8,128)(2,1)} %g_in.1, bf16[1024,128]{1,0:T(8,128)(2,1)} %wq_in.1, bf16[1024,128]{1,0:T(8,128)(2,1)} %wk_in.1, bf16[1024,128]{1,0:T(8,128)(2,1)} %wv_in.1, bf16[128,1024]{1,0:T(8,128)(2,1)} %wo_in.1, ...), custom_call_target="tpu_custom_call" | custom-call | flops 1200000000 | bytes 3000000 | tf_op jit(solution)/shard_map/pallas_call | solution.py:497
  63.7 2.1 %shard_map.120 = (bf16[256,128]{1,0:T(8,128)(2,1)}, bf16[8,128,128]{2,1,0:T(8,128)(2,1)}, bf16[8,128,128]{2,1,0:T(8,128)(2,1)}, bf16[8,128,128]{2,1,0:T(8,128)(2,1)}, bf16[128,1024]{1,0:T(8,128)(2,1)}) custom-call(bf16[256,128]{1,0:T(8,128)(2,1)} %get-tuple-element.12.ig_in, bf16[4,8,128,128]{3,2,1,0:T(8,128)(2,1)} %get-tuple-element.13.f_in), custom_call_target="tpu_custom_call" | custom-call | bytes 2200000 | tf_op jit(solution)/shard_map/pallas_call | solution.py:559

commit v5 on v4

--- a/solution.py
+++ b/solution.py
@@ -18,7 +18,7 @@
 Z_ORDER = (4, 3, 5, 2, 6, 1, 7)
 Y_ORDER = (2, 1, 3)
 X_ORDER = (2, 1, 3)
-TOPS = (64, 80)
+TOPS = (64, 96)
 PIECE = 16
 SCALE = HEAD_DIM ** (-0.5)
 BF = jnp.bfloat16
@@ -89,8 +89,8 @@
 def kernel(
     x_in, g_in, wq_in, wk_in, wv_in, wo_in, live_in, win_in,
     ig_out, f_out,
-    xg, gg, xo, go, xt, wq, wkv, w_t, wo, wo_t, kv, qs, bs, expo, ad, ad_other, late_other,
-    dkv_own, dkv_send, dkv_recv, grads,
+    xg, gg, xo, go, xt, wq, wkv, w_t, wo, wo_t, kv, qs, bs, expo, ad, ad_other,
+    dkv, dkv_other, dkv_recv, grads,
     part, ra1, rb1, ra2, rb2, fin, it_send, it_recv, it_pass, it_last, ig,
     ea1, eb1, ea2, es2, eb2, tally, live_s, win_s,
     local_sem, send_sem, recv_sem, pair_sem, out_sem,
@@ -117,6 +117,10 @@
     right = (lax.rem(node + 1, nodes), head)
     other = (node + 1 - 2 * core, head)
 
+    def along(steps):
+        return (lax.rem(node + nodes + steps, nodes), head)
+
+
     def z_dev(d):
         return ((y * NZ + at_z(d)) * 2 + core, head)
 
@@ -130,7 +134,7 @@
     mate = (node, mate_head)
 
     partners = [z_dev(d) for d in Z_ORDER] + [y_dev(d) for d in Y_ORDER]
-    partners += [x_dev(d) for d in X_ORDER] + [mate, left, right]
+    partners += [x_dev(d) for d in X_ORDER] + [mate, left, right, along(-2), along(2)]
     barrier = pltpu.get_barrier_semaphore()
     for dev in partners:
         pl.semaphore_signal(barrier, inc=1, device_id=dev, device_id_type=MESH)
@@ -250,7 +254,7 @@
     bs_t = bs[...].T
     x_core.wait()
     for s in range(SHARDS):
-        xt[s, :, ROWS:] = xo[s].T
+        xt[s, :, ROWS : 2 * ROWS] = xo[s].T
 
     def keys(i):
         return kv[i, 0:ROWS, 0:COLS]
@@ -263,33 +267,42 @@
     total = total + exponents(0) + exponents(2)
     inverse = 1.0 / total
     prob, low = {}, {}
+    mid_slot, off_slot = 2 - 2 * core, 2 * core
+    two_slots = pl.ds(1 - core, 2)
+
+    def to_other(src, dst, i):
+        return pltpu.make_async_remote_copy(
+            src_ref=src,
+            dst_ref=dst,
+            send_sem=pair_sem.at[i],
+            recv_sem=pair_sem.at[i + 1],
+            device_id=other,
+            device_id_type=MESH,
+        )
+
+    dkv_copy = to_other(dkv.at[1 - core, two_slots], dkv_other, 4)
+    early_copy = to_other(ad.at[1 - core], ad_other, 2)
     dkv_halo = copies.group()
-    for j, i, dev in ((0, 0, left), (1, 2, right)):
+    for i in (0, 2, 1):
         prob[i] = expo[i] * inverse
         low[i] = prob[i].astype(BF)
-        dkv_send[j, 1] = mm(bs_t, low[i]).astype(BF).T
-        dkv_halo.send(dkv_send.at[j, 1], dkv_recv.at[j, 1], dev)
-    prob[1] = expo[1] * inverse
+        dkv[1, i] = mm(bs_t, low[i]).astype(BF).T
+        if i == 2:
+            dkv_halo.send(dkv.at[1, off_slot], dkv_recv.at[core], along(3 * core - 1))
+
     dprob[0] = mm_nt(bs[...], vals(0))
     dprob[2] = mm_nt(bs[...], vals(2))
     delta = 0.0
     for i in range(3):
         delta = delta + jnp.sum(prob[i] * dprob[i], axis=-1, keepdims=True)
     dscore = {}
-    for j, i, dev in ((0, 0, left), (1, 2, right)):
+    for i in (0, 2, 1):
         dscore[i] = (SCALE * prob[i] * (dprob[i] - delta)).astype(BF)
-        dkv_send[j, 0] = mm(qs_t, dscore[i]).astype(BF).T
-        dkv_halo.send(dkv_send.at[j, 0], dkv_recv.at[j, 0], dev)
-
-    early_copy = pltpu.make_async_remote_copy(
-        src_ref=ad.at[1 - core],
-        dst_ref=ad_other,
-        send_sem=pair_sem.at[2],
-        recv_sem=pair_sem.at[3],
-        device_id=other,
-        device_id_type=MESH,
-    )
-    low[1] = prob[1].astype(BF)
+        dkv[0, i] = mm(qs_t, dscore[i]).astype(BF).T
+        if i == 2:
+            dkv_halo.send(dkv.at[0, off_slot], dkv_recv.at[1 - core], along(3 * core - 2))
+    dkv_copy.start()
+
     at = mm(low[0], vals(0)) + mm(low[1], vals(1)) + mm(low[2], vals(2))
     ad[1] = jnp.where(first, at[0:ROWS], at[ROWS:]).astype(BF)
 
@@ -297,7 +310,6 @@
     def _():
         early_copy.start()
 
-    dscore[1] = (SCALE * prob[1] * (dprob[1] - delta)).astype(BF)
     dq = mm(dscore[0], keys(0)) + mm(dscore[1], keys(1)) + mm(dscore[2], keys(2))
     ad[0] = jnp.where(first, dq[0:ROWS], dq[ROWS:]).astype(BF)
 
@@ -305,8 +317,6 @@
     def _():
         early_copy.start()
 
-    dkv_own[0] = mm(qs_t, dscore[1]).T
-    dkv_own[1] = mm(bs_t, low[1]).T
 
     def pair(i):
         return pl.ds(2 * i, 2)
@@ -339,16 +349,14 @@
     def spread(devices, order, ref):
         return to_all(devices, order, lambda d: ref, lambda d: ref)
 
-    def hand(e, a, b):
-        mine, top = 2 * e + core, TOPS[e]
-        group = copies.group()
-        b.wait()
-        group.send(fin.at[e, :, top:, :], f_out.at[mine, :, top:, :], other)
-        a.wait()
-        group.send(fin.at[e, :, 0:top, :], f_out.at[mine, :, 0:top, :], other)
-        out = pltpu.make_async_copy(fin.at[e], f_out.at[mine], out_sem.at[e])
+    def hand_rows(e, group, rows, i):
+        ref = f_out.at[2 * e + core]
+        group.send(fin.at[e, i, rows, :], ref.at[i, rows, :], other)
+
+    def store(e):
+        out = pltpu.make_async_copy(fin.at[e], f_out.at[2 * e + core], out_sem.at[e])
         out.start()
-        return group, out
+        return out
 
     early_copy.wait_recv()
 
@@ -371,11 +379,38 @@
             part[0, s] = mm(lhs, jnp.concatenate([gg[s], go[s]], axis=0)).astype(BF)
 
     early_a, early_b = reduce_within(0, TOPS[0], ea1, eb1)
+    dkv_copy.wait_recv()
+    own = dkv[core, 1].astype(F32) + dkv_other[core].astype(F32)
+    across = dkv[core, mid_slot].astype(F32) + dkv_other[1 - core].astype(F32)
     dkv_halo.wait()
-    for i in range(2):
-        grads[i] = (dkv_own[i] + dkv_recv[0, i].astype(F32) + dkv_recv[1, i].astype(F32)).astype(BF)
-    late_copy = copies.group().send(grads.at[1 - core], late_other, other)
-
+    grads[core] = (own + dkv_recv[0].astype(F32)).astype(BF)
+    grads[2] = (across + dkv_recv[1].astype(F32)).astype(BF)
+    rest_copy = copies.group().send(grads.at[2], grads.at[core], other)
+    part[1, :, :, :] = (
+        mm(
+            xt[...].reshape(SHARDS * COLS, 2 * ROWS),
+            jnp.concatenate([grads[core], grads[2]], axis=0),
+        )
+        .astype(BF)
+        .reshape(SHARDS, COLS, COLS)
+    )
+    late_a, late_b = reduce_within(1, TOPS[1], ra1, rb1)
+    top = TOPS[0]
+    early_a.wait()
+    ea2[y] = added(part[0, z, 0:top, :], ea1, NZ)
+    early_a = spread(y_dev, Y_ORDER, ea2.at[y])
+    early_b.wait()
+    es2[...] = added(part[0, pair(y), top:, :], eb1, NY)
+
+    def piece(i):
+        return lax.rem(i, 4) * PIECE
+
+    def es2_piece(d):
+        i = at_z(d)
+        return es2.at[i // 4, pl.ds(pl.multiple_of(piece(i), PIECE), PIECE), :]
+
+    early_b = to_all(z_dev, Z_ORDER, es2_piece, lambda d: eb2.at[d])
+    rest_copy.wait()
     all_grads = jnp.concatenate([ad[0], grads[0], grads[1]], axis=1)
     it_copies = copies.group()
     for d in X_ORDER:
@@ -384,32 +419,6 @@
         it_send[d, 1] = terms[:, COLS:]
         it_copies.send(it_send.at[d], it_recv.at[d], x_dev(d))
 
-    late_copy.wait()
-    part[1, :, :, :] = (
-        mm(
-            xt[...].reshape(SHARDS * COLS, 2 * ROWS),
-            jnp.concatenate([grads[core], late_other[...]], axis=0),
-        )
-        .astype(BF)
-        .reshape(SHARDS, COLS, COLS)
-    )
-    late_a, late_b = reduce_within(1, TOPS[1], ra1, rb1)
-
-    top = TOPS[0]
-    early_a.wait()
-    ea2[y] = added(part[0, z, 0:top, :], ea1, NZ)
-    early_a = spread(y_dev, Y_ORDER, ea2.at[y])
-    early_b.wait()
-    es2[...] = added(part[0, pair(y), top:, :], eb1, NY)
-
-    def piece(i):
-        return lax.rem(i, 4) * PIECE
-
-    def es2_piece(d):
-        i = at_z(d)
-        return es2.at[i // 4, pl.ds(pl.multiple_of(piece(i), PIECE), PIECE), :]
-
-    early_b = to_all(z_dev, Z_ORDER, es2_piece, lambda d: eb2.at[d])
 
     late_b.wait()
     rb2[z] = added(part[1, pair(y), TOPS[1] :, :], rb1, NY)
@@ -439,7 +448,8 @@
 
     late_a.wait()
     fin[1, z, 0 : TOPS[1], :] = added_in_order(ra2, NY)
-    late_a = spread(z_dev, Z_ORDER, fin.at[1, z, 0 : TOPS[1], :])
+    late_far = spread(z_dev, Z_ORDER[:3], fin.at[1, z, 0 : TOPS[1], :])
+    late_near = spread(z_dev, Z_ORDER[3:], fin.at[1, z, 0 : TOPS[1], :])
     early_b.wait()
     early_b = spread(y_dev, Y_ORDER, fin.at[0, pair(y), top:, :])
     late_b.wait()
@@ -450,12 +460,26 @@
     ig_copy = pltpu.make_async_copy(ig, ig_out, out_sem.at[2])
     ig_copy.start()
 
-    early_handed, early_out = hand(0, early_a, early_b)
-    late_handed, late_out = hand(1, late_a, late_b)
-    early_handed.wait()
-    late_handed.wait()
+    handed = copies.group()
+    tops, rests = pl.ds(0, TOPS[1]), pl.ds(TOPS[1], BLOCK - TOPS[1])
+    hand_rows(1, handed, tops, z)
+    late_near.wait()
+    for d in Z_ORDER[3:]:
+        hand_rows(1, handed, tops, at_z(d))
+    late_b.wait()
+    hand_rows(1, handed, rests, pl.ds(0, SHARDS))
+    early_b.wait()
+    early_a.wait()
+    handed.send(fin.at[0], f_out.at[core], other)
+    early_out = store(0)
+    late_far.wait()
+    for d in Z_ORDER[:3]:
+        hand_rows(1, handed, tops, at_z(d))
+    late_out = store(1)
+    handed.wait()
     copies.finish()
     early_copy.wait_send()
+    dkv_copy.wait_send()
 
     @pl.when(core == 0)
     def _():
@@ -519,11 +543,10 @@
             vm((3, 2 * ROWS, ROWS), F32),
             vm((2, ROWS, COLS), BF),
             vm((ROWS, COLS), BF),
-            vm((ROWS, COLS), BF),
-            vm((2, ROWS, COLS), F32),
-            vm((2, 2, ROWS, COLS), BF),
-            vm((2, 2, ROWS, COLS), BF),
+            vm((2, 3, ROWS, COLS), BF),
             vm((2, ROWS, COLS), BF),
+            vm((2, ROWS, COLS), BF),
+            vm((3, ROWS, COLS), BF),
             vm((2, SHARDS, BLOCK, COLS), BF),
             vm((NZ, TOPS[1], COLS), BF),
             vm((NY, 2, BLOCK - TOPS[1], COLS), BF),
@@ -546,7 +569,7 @@
             pltpu.SemaphoreType.DMA((5,)),
             pltpu.SemaphoreType.DMA((N_POOLS,)),
             pltpu.SemaphoreType.DMA((N_GROUPS,)),
-            pltpu.SemaphoreType.DMA((4,)),
+            pltpu.SemaphoreType.DMA((6,)),
             pltpu.SemaphoreType.DMA((3,)),
         ],
         compiler_params=params,

time: 65.9 us -> 64.7 us (0.982)
  Pallas kernels: 64.5 us -> 63.3 us
    pallas_call x1, Pallas kernels: 62.4 us -> 61.2 us  [body(): pl.pallas_call(kernel, out_shape=(jax.ShapeDtypeStruct((ROWS, COLS), BF),...]
where the time goes in v5:
time: 64.7 us; the launch traced here: 64.6 us
  Pallas kernels  63.3 us (98%)
  between operations  1.29 us (2%)
    pallas_call x1, Pallas kernels, body(): pl.pallas_call(kernel, out_shape=(jax.ShapeDtypeStruct((ROWS, COLS), BF),...  61.2 us
    pallas_call x1, Pallas kernels, body(): pl.pallas_call(hand_out, out_shape=(jax.ShapeDtypeStruct((ROWS, COLS), BF...  2.07 us

profile of v5, /device:TPU:1, one launch (start us, length us, event | category | flops | bytes accessed | tf_op | source)
XLA Modules:
  0.0 64.6 jit_solution(8794082284802421233)
XLA Ops:
  1.3 61.2 %shard_map.119 = (bf16[256,128]{1,0:T(8,128)(2,1)}, bf16[4,8,128,128]{3,2,1,0:T(8,128)(2,1)}) custom-call(bf16[256,128]{1,0:T(8,128)(2,1)} %x_in.1, bf16[256,128]{1,0:T(8,128)(2,1)} %g_in.1, bf16[1024,128]{1,0:T(8,128)(2,1)} %wq_in.1, bf16[1024,128]{1,0:T(8,128)(2,1)} %wk_in.1, bf16[1024,128]{1,0:T(8,128)(2,1)} %wv_in.1, bf16[128,1024]{1,0:T(8,128)(2,1)} %wo_in.1, ...), custom_call_target="tpu_custom_call" | custom-call | flops 1200000000 | bytes 3000000 | tf_op jit(solution)/shard_map/pallas_call | solution.py:521
  62.5 2.1 %shard_map.120 = (bf16[256,128]{1,0:T(8,128)(2,1)}, bf16[8,128,128]{2,1,0:T(8,128)(2,1)}, bf16[8,128,128]{2,1,0:T(8,128)(2,1)}, bf16[8,128,128]{2,1,0:T(8,128)(2,1)}, bf16[128,1024]{1,0:T(8,128)(2,1)}) custom-call(bf16[256,128]{1,0:T(8,128)(2,1)} %get-tuple-element.12.ig_in, bf16[4,8,128,128]{3,2,1,0:T(8,128)(2,1)} %get-tuple-element.13.f_in), custom_call_target="tpu_custom_call" | custom-call | bytes 2200000 | tf_op jit(solution)/shard_map/pallas_call | solution.py:582

commit v6 on v5

--- a/solution.py
+++ b/solution.py
@@ -20,6 +20,7 @@
 X_ORDER = (2, 1, 3)
 TOPS = (64, 96)
 PIECE = 16
+LATE_PART = TOPS[1] // 2
 SCALE = HEAD_DIM ** (-0.5)
 BF = jnp.bfloat16
 F32 = jnp.float32
@@ -349,10 +350,6 @@
     def spread(devices, order, ref):
         return to_all(devices, order, lambda d: ref, lambda d: ref)
 
-    def hand_rows(e, group, rows, i):
-        ref = f_out.at[2 * e + core]
-        group.send(fin.at[e, i, rows, :], ref.at[i, rows, :], other)
-
     def store(e):
         out = pltpu.make_async_copy(fin.at[e], f_out.at[2 * e + core], out_sem.at[e])
         out.start()
@@ -394,7 +391,19 @@
         .astype(BF)
         .reshape(SHARDS, COLS, COLS)
     )
-    late_a, late_b = reduce_within(1, TOPS[1], ra1, rb1)
+    def late_part(i):
+        return slice(i * LATE_PART, (i + 1) * LATE_PART)
+
+    def late_reduce(i):
+        return to_all(
+            z_dev, Z_ORDER, lambda d: part.at[1, at_z(d), late_part(i), :], lambda d: ra1.at[i, d]
+        )
+
+    late_0 = late_reduce(0)
+    late_b = to_all(
+        y_dev, Y_ORDER, lambda d: part.at[1, pair(at_y(d)), TOPS[1] :, :], lambda d: rb1.at[d]
+    )
+    late_1 = late_reduce(1)
     top = TOPS[0]
     early_a.wait()
     ea2[y] = added(part[0, z, 0:top, :], ea1, NZ)
@@ -423,9 +432,16 @@
     late_b.wait()
     rb2[z] = added(part[1, pair(y), TOPS[1] :, :], rb1, NY)
     late_b = spread(z_dev, Z_ORDER, rb2.at[z])
-    late_a.wait()
-    ra2[y] = added(part[1, z, 0 : TOPS[1], :], ra1, NZ)
-    late_a = spread(y_dev, Y_ORDER, ra2.at[y])
+    def late_exchange(i):
+        ra2[i, y] = added(part[1, z, late_part(i), :], ra1.at[i], NZ)
+        return spread(y_dev, Y_ORDER, ra2.at[i, y])
+
+    def late_gather(i):
+        fin[1, z, late_part(i), :] = added_in_order(ra2.at[i], NY)
+        return spread(z_dev, Z_ORDER, fin.at[1, z, late_part(i), :])
+
+    late_0.wait()
+    late_0 = late_exchange(0)
 
     early_b.wait()
     own_piece = pl.ds(pl.multiple_of(piece(z), PIECE), PIECE)
@@ -435,6 +451,18 @@
     early_a.wait()
     fin[0, z, 0:top, :] = added_in_order(ea2, NY)
     early_a = spread(z_dev, Z_ORDER, fin.at[0, z, 0:top, :])
+    late_1.wait()
+    late_1 = late_exchange(1)
+
+    late_0.wait()
+    late_0 = late_gather(0)
+    early_b.wait()
+    early_b = spread(y_dev, Y_ORDER, fin.at[0, pair(y), top:, :])
+    late_b.wait()
+    fin[1, pair(y), TOPS[1] :, :] = added_in_order(rb2, NZ)
+    late_b = spread(y_dev, Y_ORDER, fin.at[1, pair(y), TOPS[1] :, :])
+    late_1.wait()
+    late_1 = late_gather(1)
 
     it_own = mm(all_grads, w_t[xx])
     low_half, high_half = it_own[:, 0:COLS], it_own[:, COLS:]
@@ -446,35 +474,27 @@
     it_pass[...] = jnp.where(is_low, high_half, low_half).astype(BF)
     it_copy = copies.group().send(it_pass, it_last, mate)
 
-    late_a.wait()
-    fin[1, z, 0 : TOPS[1], :] = added_in_order(ra2, NY)
-    late_far = spread(z_dev, Z_ORDER[:3], fin.at[1, z, 0 : TOPS[1], :])
-    late_near = spread(z_dev, Z_ORDER[3:], fin.at[1, z, 0 : TOPS[1], :])
-    early_b.wait()
-    early_b = spread(y_dev, Y_ORDER, fin.at[0, pair(y), top:, :])
-    late_b.wait()
-    fin[1, pair(y), TOPS[1] :, :] = added_in_order(rb2, NZ)
-    late_b = spread(y_dev, Y_ORDER, fin.at[1, pair(y), TOPS[1] :, :])
     it_copy.wait()
     ig[...] = (jnp.where(is_low, low_half, high_half) + it_last[...].astype(F32)).astype(BF)
     ig_copy = pltpu.make_async_copy(ig, ig_out, out_sem.at[2])
     ig_copy.start()
 
     handed = copies.group()
-    tops, rests = pl.ds(0, TOPS[1]), pl.ds(TOPS[1], BLOCK - TOPS[1])
-    hand_rows(1, handed, tops, z)
-    late_near.wait()
-    for d in Z_ORDER[3:]:
-        hand_rows(1, handed, tops, at_z(d))
+
+    def hand(e, rows):
+        handed.send(fin.at[e, :, rows, :], f_out.at[2 * e + core, :, rows, :], other)
+
+    early_a.wait()
+    hand(0, slice(0, top))
     late_b.wait()
-    hand_rows(1, handed, rests, pl.ds(0, SHARDS))
+    hand(1, slice(TOPS[1], BLOCK))
+    late_0.wait()
+    hand(1, late_part(0))
     early_b.wait()
-    early_a.wait()
-    handed.send(fin.at[0], f_out.at[core], other)
+    hand(0, slice(top, BLOCK))
     early_out = store(0)
-    late_far.wait()
-    for d in Z_ORDER[:3]:
-        hand_rows(1, handed, tops, at_z(d))
+    late_1.wait()
+    hand(1, late_part(1))
     late_out = store(1)
     handed.wait()
     copies.finish()
@@ -490,7 +510,7 @@
 
 
 POOL_ROWS = 2560
-N_GROUPS = 27
+N_GROUPS = 29
 N_POOLS = 7
 
 
@@ -548,9 +568,9 @@
             vm((2, ROWS, COLS), BF),
             vm((3, ROWS, COLS), BF),
             vm((2, SHARDS, BLOCK, COLS), BF),
-            vm((NZ, TOPS[1], COLS), BF),
+            vm((2, NZ, LATE_PART, COLS), BF),
             vm((NY, 2, BLOCK - TOPS[1], COLS), BF),
-            vm((NY, TOPS[1], COLS), BF),
+            vm((2, NY, LATE_PART, COLS), BF),
             vm((NZ, 2, BLOCK - TOPS[1], COLS), BF),
             vm((2, SHARDS, BLOCK, COLS), BF),
             vm((NX, 2, ROWS, COLS), BF),

time: 64.7 us -> 64.4 us (level)
  no operation moved by 1% of the time
where the time goes in v6:
time: 64.4 us; the launch traced here: 64.3 us
  Pallas kernels  63 us (98%)
  between operations  1.29 us (2%)
    pallas_call x1, Pallas kernels, body(): pl.pallas_call(kernel, out_shape=(jax.ShapeDtypeStruct((ROWS, COLS), BF),...  60.9 us
    pallas_call x1, Pallas kernels, body(): pl.pallas_call(hand_out, out_shape=(jax.ShapeDtypeStruct((ROWS, COLS), BF...  2.07 us

profile of v6, /device:TPU:1, one launch (start us, length us, event | category | flops | bytes accessed | tf_op | source)
XLA Modules:
  0.0 64.3 jit_solution(13472859655481846778)
XLA Ops:
  1.3 60.9 %shard_map.119 = (bf16[256,128]{1,0:T(8,128)(2,1)}, bf16[4,8,128,128]{3,2,1,0:T(8,128)(2,1)}) custom-call(bf16[256,128]{1,0:T(8,128)(2,1)} %x_in.1, bf16[256,128]{1,0:T(8,128)(2,1)} %g_in.1, bf16[1024,128]{1,0:T(8,128)(2,1)} %wq_in.1, bf16[1024,128]{1,0:T(8,128)(2,1)} %wk_in.1, bf16[1024,128]{1,0:T(8,128)(2,1)} %wv_in.1, bf16[128,1024]{1,0:T(8,128)(2,1)} %wo_in.1, ...), custom_call_target="tpu_custom_call" | custom-call | flops 1200000000 | bytes 3000000 | tf_op jit(solution)/shard_map/pallas_call | solution.py:541
  62.2 2.1 %shard_map.120 = (bf16[256,128]{1,0:T(8,128)(2,1)}, bf16[8,128,128]{2,1,0:T(8,128)(2,1)}, bf16[8,128,128]{2,1,0:T(8,128)(2,1)}, bf16[8,128,128]{2,1,0:T(8,128)(2,1)}, bf16[128,1024]{1,0:T(8,128)(2,1)}) custom-call(bf16[256,128]{1,0:T(8,128)(2,1)} %get-tuple-element.12.ig_in, bf16[4,8,128,128]{3,2,1,0:T(8,128)(2,1)} %get-tuple-element.13.f_in), custom_call_target="tpu_custom_call" | custom-call | bytes 2200000 | tf_op jit(solution)/shard_map/pallas_call | solution.py:602

commit v7 on v6

--- a/solution.py
+++ b/solution.py
@@ -185,10 +185,6 @@
     g_mate.wait()
     for d in (1, 3):
         g_rest.send(gg.at[mate_head], gg.at[mate_head], x_dev(d))
-    for s in range(SHARDS):
-        rows, cols = slice(s * COLS, (s + 1) * COLS), slice((s % 2) * COLS, (s % 2 + 1) * COLS)
-        w_t[s // 2, 0:COLS, cols] = wq[rows, :].T
-        w_t[s // 2, COLS:, cols] = wkv[rows, :].T
     x_rest.wait()
 
     x_full = jnp.concatenate([xg[s] for s in range(SHARDS)], axis=1)
@@ -379,6 +375,10 @@
     dkv_copy.wait_recv()
     own = dkv[core, 1].astype(F32) + dkv_other[core].astype(F32)
     across = dkv[core, mid_slot].astype(F32) + dkv_other[1 - core].astype(F32)
+    for s in range(SHARDS):
+        rows, cols = slice(s * COLS, (s + 1) * COLS), slice((s % 2) * COLS, (s % 2 + 1) * COLS)
+        w_t[s // 2, 0:COLS, cols] = wq[rows, :].T
+        w_t[s // 2, COLS:, cols] = wkv[rows, :].T
     dkv_halo.wait()
     grads[core] = (own + dkv_recv[0].astype(F32)).astype(BF)
     grads[2] = (across + dkv_recv[1].astype(F32)).astype(BF)

time: 64.4 us -> 64.4 us (level)
  no operation moved by 1% of the time
where the time goes in v7:
time: 64.4 us; the launch traced here: 64.3 us
  Pallas kernels  63 us (98%)
  between operations  1.29 us (2%)
    pallas_call x1, Pallas kernels, body(): pl.pallas_call(kernel, out_shape=(jax.ShapeDtypeStruct((ROWS, COLS), BF),...  60.9 us
    pallas_call x1, Pallas kernels, body(): pl.pallas_call(hand_out, out_shape=(jax.ShapeDtypeStruct((ROWS, COLS), BF...  2.07 us

profile of v7, /device:TPU:1, one launch (start us, length us, event | category | flops | bytes accessed | tf_op | source)
XLA Modules:
  0.0 64.3 jit_solution(12214807362333807725)
XLA Ops:
  1.3 60.9 %shard_map.119 = (bf16[256,128]{1,0:T(8,128)(2,1)}, bf16[4,8,128,128]{3,2,1,0:T(8,128)(2,1)}) custom-call(bf16[256,128]{1,0:T(8,128)(2,1)} %x_in.1, bf16[256,128]{1,0:T(8,128)(2,1)} %g_in.1, bf16[1024,128]{1,0:T(8,128)(2,1)} %wq_in.1, bf16[1024,128]{1,0:T(8,128)(2,1)} %wk_in.1, bf16[1024,128]{1,0:T(8,128)(2,1)} %wv_in.1, bf16[128,1024]{1,0:T(8,128)(2,1)} %wo_in.1, ...), custom_call_target="tpu_custom_call" | custom-call | flops 1200000000 | bytes 3000000 | tf_op jit(solution)/shard_map/pallas_call | solution.py:541
  62.2 2.1 %shard_map.120 = (bf16[256,128]{1,0:T(8,128)(2,1)}, bf16[8,128,128]{2,1,0:T(8,128)(2,1)}, bf16[8,128,128]{2,1,0:T(8,128)(2,1)}, bf16[8,128,128]{2,1,0:T(8,128)(2,1)}, bf16[128,1024]{1,0:T(8,128)(2,1)}) custom-call(bf16[256,128]{1,0:T(8,128)(2,1)} %get-tuple-element.12.ig_in, bf16[4,8,128,128]{3,2,1,0:T(8,128)(2,1)} %get-tuple-element.13.f_in), custom_call_target="tpu_custom_call" | custom-call | bytes 2200000 | tf_op jit(solution)/shard_map/pallas_call | solution.py:602
